TPU v7x, 32 devices: a whole 2x2x4 slice. The times are simulated.
32 devices in a mesh: frames: 16 (over z, y, x), coils: 2 (over core).
Axes of the slice: x: 2, y: 2, z: 4, core: 2. Of those that a mesh axis runs over, the one named last changes fastest.
Arguments:
- kspace: bfloat16 [16, 8, 2, 32, 256], P('frames', 'coils'), may hold values from -6 to 6
- sensitivity: bfloat16 [8, 2, 256, 256], P('coils'), may hold values from -3 to 3
- spoke_count: int32 [16], P('frames'), may hold values from 1 to 32, 384 in all
- spoke_index: int32 [16, 32], P('frames'), may hold values from 0 to 32767
- band_offset: int32 [16, 32], P('frames'), may hold values from 0 to 252
- owner_map: int32 [2, 32768], replicated, may hold values from 0 to 32767, each once within a row
- aif: float32 [16], replicated, may hold values from 0.2 to 5
- ktrans: float32 [2, 32768], P('coils', 'frames'), may hold values from 0.02 to 0.4
- kep: float32 [2, 32768], P('coils', 'frames'), may hold values from 0.1 to 2
- baseline: float32 [2, 2, 32768], P(None, 'coils', 'frames'), may hold values from 0.5 to 2
Outputs:
- ktrans_new: float32 [2, 32768], P('coils', 'frames')
- kep_new: float32 [2, 32768], P('coils', 'frames')
- residual_images: bfloat16 [16, 2, 256, 256], P('frames', None, 'coils')
Inputs may be any that keep to these rules, and one draw needn't show every extreme that they name: `spoke_count`: spoke counts of all frames sum to 384; some frame uses all 32 slots. `owner_map`: each row is a permutation of 0 to 32767.
All inputs are finite; a program needn't handle non-finite values. No bound on the sum of `spoke_count` on one device may be relied on, other than what follows from the above.
Results may differ from a plain program's by a relative error of at most 0.0074.
Values may be sent and summed in bfloat16 or wider, within the bound.
A program may use at most 64 MiB of HBM per device.

v0:
```python
import math

import jax
import jax.numpy as jnp
from jax import lax
from jax.sharding import PartitionSpec as P

KERNEL = (0.25, 0.75, 0.75, 0.25)
STEP_MINUTES = 0.05
DAMPING = 0.1


def dft_tables(length):
    index = jnp.arange(length, dtype=jnp.int32)
    phase = (index[:, None] * index[None, :] % length).astype(jnp.float32) * (
        2.0 * math.pi / length
    )
    norm = 1.0 / math.sqrt(length)
    cosine = (jnp.cos(phase) * norm).astype(jnp.bfloat16)
    sine = (jnp.sin(phase) * norm).astype(jnp.bfloat16)
    column_table = jnp.stack([jnp.stack([cosine, sine], 1), jnp.stack([-sine, cosine], 1)], 0)
    row_table = jnp.stack([jnp.stack([cosine, -sine], 1), jnp.stack([sine, cosine], 1)], 0)
    return (column_table, row_table)


def spoke_weights(count, offset, spoke_number, rows):
    spokes = offset.shape[0]
    row_ids = jnp.arange(rows, dtype=jnp.int32)
    band = jnp.zeros((rows, spokes), jnp.float32)
    for shift_b in range(len(KERNEL)):
        band = band + KERNEL[shift_b] * (row_ids[:, None] == offset[None, :] + shift_b).astype(
            jnp.float32
        )
    live = (jnp.arange(spokes, dtype=jnp.int32) < count).astype(jnp.float32)
    turn = (spoke_number * 40503 % 65536).astype(jnp.float32) * (2.0 * math.pi / 65536.0)
    w_cos = band * (live * jnp.cos(turn))[None, :]
    w_sin = band * (live * jnp.sin(turn))[None, :]
    return jnp.stack([jnp.stack([w_cos, -w_sin], 1), jnp.stack([w_sin, w_cos], 1)], 0).astype(
        jnp.bfloat16
    )


def aif_matrix(aif):
    length = aif.shape[0]
    index = jnp.arange(length, dtype=jnp.int32)
    lag = index[:, None] - index[None, :]
    table = jnp.take(aif, jnp.clip(lag, 0, length - 1))
    return jnp.where(lag >= 0, table, jnp.zeros_like(table)) * STEP_MINUTES


def tofts_step(images, aif, ktrans, kep, baseline):
    frames = images.shape[0]
    times = jnp.arange(frames, dtype=jnp.int32).astype(jnp.float32) * STEP_MINUTES
    toeplitz = aif_matrix(aif)
    decay = jnp.exp(-times[:, None] * kep[None, :])
    conc = jnp.dot(toeplitz, decay, precision=lax.Precision.HIGHEST)
    slope = jnp.dot(toeplitz, -times[:, None] * decay, precision=lax.Precision.HIGHEST)
    real_part = images[:, 0]
    imag_part = images[:, 1]
    base_r = baseline[0][None, :]
    base_i = baseline[1][None, :]
    scale = 1.0 + ktrans[None, :] * conc
    miss_r = real_part - base_r * scale
    miss_i = imag_part - base_i * scale
    power = baseline[0] * baseline[0] + baseline[1] * baseline[1]
    project = base_r * miss_r + base_i * miss_i
    h_aa = power * jnp.sum(conc * conc, 0)
    h_ab = power * ktrans * jnp.sum(conc * slope, 0)
    h_bb = power * ktrans * ktrans * jnp.sum(slope * slope, 0)
    g_a = jnp.sum(conc * project, 0)
    g_b = ktrans * jnp.sum(slope * project, 0)
    d_aa = (1.0 + DAMPING) * h_aa + 1.0
    d_bb = (1.0 + DAMPING) * h_bb + 1.0
    determinant = d_aa * d_bb - h_ab * h_ab
    kt_next = ktrans + (d_bb * g_a - h_ab * g_b) / determinant
    kp_next = kep + (d_aa * g_b - h_ab * g_a) / determinant
    conc_next = jnp.dot(
        toeplitz, jnp.exp(-times[:, None] * kp_next[None, :]), precision=lax.Precision.HIGHEST
    )
    scale_next = 1.0 + kt_next[None, :] * conc_next
    residual = jnp.stack([real_part - base_r * scale_next, imag_part - base_i * scale_next], 1)
    return (kt_next, kp_next, residual)


def full_partial(row_table, half, sensitivity):
    coil_image = jnp.einsum(
        "qypr,fcprx->fcqyx", row_table, half, preferred_element_type=jnp.float32
    )
    sens = sensitivity.astype(jnp.float32)[None]
    partial_r = jnp.sum(
        sens[:, :, 0] * coil_image[:, :, 0] + sens[:, :, 1] * coil_image[:, :, 1], 1
    )
    partial_i = jnp.sum(
        sens[:, :, 0] * coil_image[:, :, 1] - sens[:, :, 1] * coil_image[:, :, 0], 1
    )
    return jnp.stack([partial_r, partial_i], 1)


def shards(
    kspace,
    sensitivity,
    spoke_count,
    spoke_index,
    band_offset,
    owner_map,
    aif,
    ktrans,
    kep,
    baseline,
):
    frame_dev, coil_dev, _, spokes, width = kspace.shape
    n_coils = lax.axis_size("coils")
    slab_vox = owner_map.shape[1]
    vox_dev = ktrans.shape[1]
    column_table, row_table = dft_tables(width)
    weights = jax.vmap(spoke_weights, in_axes=(0, 0, 0, None))(
        spoke_count, band_offset, spoke_index, width
    )
    grid = jnp.einsum("fqxps,fcpsy->fcqxy", weights, kspace, preferred_element_type=jnp.float32)
    grid = grid.astype(jnp.bfloat16)
    half = jnp.einsum(
        "fcprk,pkqx->fcqrx", grid, column_table, preferred_element_type=jnp.float32
    ).astype(jnp.bfloat16)
    coil_row = lax.dynamic_index_in_dim(owner_map, lax.axis_index("coils"), 0, keepdims=False)
    partial_value = full_partial(row_table, half, sensitivity)
    summed = lax.psum_scatter(partial_value, "coils", scatter_dimension=2, tiled=True)
    slab = summed.astype(jnp.bfloat16).reshape(frame_dev, 2, slab_vox)
    picked = jnp.take(slab, coil_row, axis=2)
    owned = lax.all_to_all(picked, "frames", split_axis=2, concat_axis=0, tiled=True)
    kt_next, kp_next, residual = tofts_step(
        owned.astype(jnp.float32), aif, ktrans[0], kep[0], baseline[:, 0]
    )
    returned = lax.all_to_all(
        residual.astype(jnp.bfloat16), "frames", split_axis=0, concat_axis=2, tiled=True
    )
    placed = jnp.zeros_like(returned).at[:, :, coil_row].set(returned)
    return (
        kt_next.reshape(1, vox_dev),
        kp_next.reshape(1, vox_dev),
        placed.reshape(frame_dev, 2, width // n_coils, width),
    )


def solution(mesh):
    in_specs = (
        P("frames", "coils", None, None, None),
        P("coils", None, None, None),
        P("frames"),
        P("frames", None),
        P("frames", None),
        P(),
        P(),
        P("coils", "frames"),
        P("coils", "frames"),
        P(None, "coils", "frames"),
    )
    out_specs = (P("coils", "frames"), P("coils", "frames"), P("frames", None, "coils", None))
    return jax.shard_map(shards, mesh=mesh, in_specs=in_specs, out_specs=out_specs, check_vma=False)
```

profile of v0, /device:TPU:0, one launch (start us, length us, event | category | flops | bytes accessed | tf_op | source)
XLA Modules:
  0.0 676.5 jit_solution(8298726999160821806)
XLA Ops:
  7.2 0.0 copy-start
  7.2 0.0 reduce-scatter.2.cloned.1.call-start
  7.2 1.1 multiply_convert_fusion
  8.3 1.0 fusion.42
  10.0 0.7 broadcast_add_fusion.2
  10.7 1.5 copy.55
  12.1 0.2 bitcast_convert_fusion.2
  12.3 0.7 fusion.51
  13.1 0.0 copy-start.3
  13.1 0.1 fusion.15
  13.2 0.0 copy-start.4
  13.2 0.8 negate_convert_fusion
  13.9 0.0 copy-done
  14.0 0.5 fusion.3
  14.4 0.7 fusion.4
  15.2 0.7 convolution_bitcast_fusion
  15.9 0.4 add_reduce_fusion
  16.3 0.1 copy.60
  16.4 0.1 copy.61
  16.5 0.8 pad_maximum_fusion
  17.4 0.0 reduce-scatter.2.cloned.1.call-update
  17.4 0.0 copy-done.3
  17.4 0.2 compare_select_fusion
  17.7 0.0 copy-done.4
  17.7 0.1 reshape.983
  17.8 10.4 %reduce-scatter.2.cloned.1.call-done = f32[1,2,128,256]{3,2,1,0:T(8,128)} async-done(((f32[1,2,256,256]{3,2,1,0:T(8,128)}), f32[1,2,128,256]{3,2,1,0:T(8,128)}) %reduce-scatter.2.cloned.1.call-update) | async-done | bytes 262160 | tf_op jit(solution)/shard_map/reduce_scatter | solution.py:126
  28.2 1.0 convert_element_type.142
  29.1 6.1 copy.62
  35.3 113.8 %gather_fusion.1 = bf16[32768,2]{1,0:T(8,128)(2,1)} fusion(bf16[2,32768]{0,1:T(8,128)(2,1)} %bitcast.178, s32[32768]{0:T(1024)S(1)} %broadcast_clamp_fusion), kind=kCustom, calls=%fused_computation.1 | custom fusion | bytes 393216 | tf_op jit(solution)/shard_map/jit(_take)/gather | solution.py:128
  149.1 18.4 %bitcast_select_fusion = bf16[1,2,32768]{1,2,0:T(8,128)(2,1)S(1)} fusion(bf16[32768,2]{1,0:T(8,128)(2,1)} %gather_fusion.1, pred[32768]{0:T(1024)(128)(4,1)S(1)} %compare_and_fusion), kind=kLoop, calls=%fused_computation.3 | loop fusion | flops 65536 | bytes 294912 | tf_op jit(solution)/shard_map/jit(_take)/select_n | solution.py:128
  167.5 130.9 %copy.88 = bf16[1,2,32768]{1,0,2:T(2,128)(2,1)} copy(bf16[1,2,32768]{1,2,0:T(8,128)(2,1)S(1)} %bitcast_select_fusion) | data formatting | bytes 262144 | tf_op jit(solution)/shard_map/jit(_take)/select_n | solution.py:128
  298.4 0.5 broadcast.970
  298.9 179.1 %reduce.4 = bf16[32768,2]{1,0:T(8,128)(2,1)} reduce(bf16[32768,1,2]{2,1,0:T(2,128)(2,1)} %bitcast.175, bf16[]{:T(256)} %broadcast.970), dimensions={1}, to_apply=%bitcast.172.reduce_sub_computation | reduce | bytes 262146
  478.0 0.0 copy-start.2
  478.0 0.0 copy-start.5
  478.0 13.8 %reshape.1024 = bf16[16,2,2048]{2,1,0:T(2,128)(2,1)} reshape(bf16[32768,2]{1,0:T(8,128)(2,1)} %reduce.4) | data formatting | bytes 262144
  491.8 6.8 %all-to-all-start = ((bf16[16,2,2048]{2,1,0:T(2,128)(2,1)}), bf16[16,2,2048]{2,1,0:T(2,128)(2,1)S(1)}, u32[]{:S(2)}, u32[]{:S(2)}) async-start(bf16[16,2,2048]{2,1,0:T(2,128)(2,1)} %reshape.1024), calls=%async_computation.1 | async-start | bytes 262144 | tf_op jit(solution)/shard_map/all_to_all | solution.py:129
  498.6 0.0 copy-done.2
  498.6 1.9 gather_fusion
  500.5 0.1 reshape.982
  500.5 0.0 copy-done.5
  500.5 0.3 fusion.27
  500.9 5.6 all-to-all-done
  506.5 20.8 %reshape.1025 = bf16[32768,1,2]{2,1,0:T(2,128)(2,1)} reshape(bf16[16,2,2048]{2,1,0:T(2,128)(2,1)S(1)} %all-to-all-done) | data formatting | bytes 262144
  527.3 0.0 copy-start.6
  527.3 30.6 %copy.64 = bf16[1,2,32768]{2,1,0:T(2,128)(2,1)S(1)} copy(bf16[1,2,32768]{1,0,2:T(2,128)(2,1)} %bitcast.176) | data formatting | bytes 262144 | tf_op jit(solution)/shard_map/all_to_all | solution.py:129
  557.9 0.1 copy.87
  557.9 0.0 copy-done.6
  557.9 0.4 multiply_reduce_fusion.1
  558.3 0.1 divide_add_fusion
  558.4 0.0 copy-start.7
  558.4 0.0 copy-start.8
  558.4 0.4 fusion.28
  558.8 0.1 copy.65
  559.0 10.8 %all_to_all.27 = bf16[16,2,2048]{2,1,0:T(2,128)(2,1)S(1)} all-to-all(bf16[16,2,2048]{2,1,0:T(2,128)(2,1)S(1)} %copy.65), channel_id=1, replica_groups=mesh['frames'=16,'coils'=2] {'frames'}, dimensions={0} | all-to-all | bytes 262144 | tf_op jit(solution)/shard_map/all_to_all | solution.py:133
  569.7 0.0 copy-start.1
  569.7 5.5 copy.66
  575.3 86.5 %scatter_custom_fusion = bf16[2,32768]{0,1:T(8,128)(2,1)} fusion(s32[32768]{0:T(1024)S(1)} %bitcast.185, bf16[32768,2]{1,0:T(8,128)(2,1)} %copy.66, bf16[]{:T(256)} %constant.108.clone.1), kind=kCustom, calls=%fused_computation.4 | custom fusion | bytes 131584 | tf_op jit(solution)/shard_map/scatter | solution.py:136
  661.8 0.0 copy-done.7
  661.8 0.0 copy-done.8
  661.8 7.9 %copy.67 = bf16[1,2,128,256]{3,2,1,0:T(8,128)(2,1)} copy(bf16[1,2,128,256]{1,3,2,0:T(8,128)(2,1)} %bitcast.177) | data formatting | bytes 262144
  669.7 0.0 copy-done.1
  (8 shorter events, 0.1 us)
Async XLA Ops:
  7.2 6.8 %copy-start = (bf16[1,4,2,32,256]{4,3,2,1,0:T(8,128)(2,1)S(1)}, bf16[1,4,2,32,256]{4,3,2,1,0:T(8,128)(2,1)}, u32[]{:S(2)}) copy-start(bf16[1,4,2,32,256]{4,3,2,1,0:T(8,128)(2,1)} %param.10) | copy-start | bytes 393220
  7.2 21.0 %reduce-scatter.2.cloned.1.call-start = ((), (), s32[]{:S(2)}) async-start(), calls=%async_computation.3 | async-start | bytes 786432 | tf_op jit(solution)/shard_map/reduce_scatter | solution.py:126
  13.1 4.3 copy-start.3
  13.2 4.5 copy-start.4
  478.0 20.6 %copy-start.2 = (f32[16]{0:T(128)S(1)}, f32[16]{0:T(128)}, u32[]{:S(2)}) copy-start(f32[16]{0:T(128)} %param.16) | copy-start | bytes 196
  478.0 22.5 %copy-start.5 = (f32[1,2048]{1,0:T(1,128)S(1)}, f32[1,2048]{1,0:T(1,128)}, u32[]{:S(2)}) copy-start(f32[1,2048]{1,0:T(1,128)} %param.18) | copy-start | bytes 24580
  491.8 14.7 %all-to-all-start = ((bf16[16,2,2048]{2,1,0:T(2,128)(2,1)}), bf16[16,2,2048]{2,1,0:T(2,128)(2,1)S(1)}, u32[]{:S(2)}, u32[]{:S(2)}) async-start(bf16[16,2,2048]{2,1,0:T(2,128)(2,1)} %reshape.1024), calls=%async_computation.1 | async-start | bytes 262144 | tf_op jit(solution)/shard_map/all_to_all | solution.py:129
  527.3 30.6 %copy-start.6 = (f32[1,2048]{1,0:T(1,128)S(1)}, f32[1,2048]{1,0:T(1,128)}, u32[]{:S(2)}) copy-start(f32[1,2048]{1,0:T(1,128)} %param.17) | copy-start | bytes 24580
  558.4 103.4 %copy-start.7 = (f32[1,2048]{1,0:T(1,128)}, f32[1,2048]{1,0:T(1,128)S(1)}, u32[]{:S(2)}) copy-start(f32[1,2048]{1,0:T(1,128)S(1)} %get-tuple-element.37) | copy-start | bytes 24580
  558.4 103.4 %copy-start.8 = (f32[1,2048]{1,0:T(1,128)}, f32[1,2048]{1,0:T(1,128)S(1)}, u32[]{:S(2)}) copy-start(f32[1,2048]{1,0:T(1,128)S(1)} %get-tuple-element.38) | copy-start | bytes 24580
  569.7 99.9 %copy-start.1 = (bf16[1,4,2,32,256]{4,3,2,1,0:T(8,128)(2,1)S(1)}, bf16[1,4,2,32,256]{4,3,2,1,0:T(8,128)(2,1)}, u32[]{:S(2)}) copy-start(bf16[1,4,2,32,256]{4,3,2,1,0:T(8,128)(2,1)} %param.10) | copy-start | bytes 393220
Sparse Core Ops, SparseCore 0:
  17.5 10.6 reduce-scatter.1
where the time goes:
time: 678 us; the launch traced here: 677 us
  local copies, waits for them, and re-layouts  420 us (62%)
  other arithmetic  205 us (30%)
  waiting for transfers between devices  16 us (2%)
  between operations  15 us (2%)
  blocking collectives  10.8 us (2%)
  starting transfers between devices  6.81 us (1%)
    unnamed x1, other arithmetic  179 us
    select_n x1, local copies, waits for them, and re-layouts, shards(): picked = jnp.take(slab, coil_row, axis=2)  131 us
    gather x1, local copies, waits for them, and re-layouts, shards(): picked = jnp.take(slab, coil_row, axis=2)  114 us
    scatter x1, local copies, waits for them, and re-layouts, shards(): placed = jnp.zeros_like(returned).at[:, :, coil_row].set(returned)  86.5 us
    unnamed x24, local copies, waits for them, and re-layouts  44.5 us
    all_to_all x1, local copies, waits for them, and re-layouts, shards(): lax.all_to_all(picked, 'frames', split_axis=2, concat_axis=0, tiled=True)  30.6 us
    select_n x2, other arithmetic, shards(): picked = jnp.take(slab, coil_row, axis=2)  18.6 us
  transfers between devices with their start and end apart: 2, of which 2 were waited for; matrix products, arithmetic and copies ran while one was open for 0% of the time, Pallas kernels for 0%

commit v1 on v0

v1 whole, which is shorter than its diff:
```python
import functools
import math

import jax
import jax.numpy as jnp
import numpy as np
from jax import lax
from jax.experimental import pallas as pl
from jax.experimental.pallas import tpu as pltpu
from jax.sharding import PartitionSpec as P

STEP_MINUTES = 0.05
DAMPING = 0.1
LANES = 128
MESH = pl.DeviceIdType.MESH
F32 = jnp.float32
BF16 = jnp.bfloat16
NT = (((1,), (1,)), ((), ()))


def dft_table(length):
    index = np.arange(length, dtype=np.int64)
    phase = (index[:, None] * index[None, :] % length) * (2.0 * math.pi / length)
    table = np.concatenate([np.cos(phase), np.sin(phase)], 1) / math.sqrt(length)
    return jnp.asarray(table.astype(np.float32)).astype(BF16)


class Chunks:
    def __init__(self, width, voxels):
        self.columns = min(width, voxels)
        self.rows = voxels // self.columns
        self.parts = width // self.columns
        self.height = voxels // LANES

    def pieces(self, number):
        row = number // self.parts * self.rows
        column = number % self.parts * self.columns
        for lane in range(0, self.columns, LANES):
            yield row, slice(column + lane, column + lane + LANES)

    def take(self, plane, number):
        return [plane[row : row + self.rows, lanes] for row, lanes in self.pieces(number)]


def kernel(
    n_frames,
    n_coils,
    kspace,
    sens,
    count,
    spoke_index,
    offset,
    owner,
    aif,
    ktrans,
    kep,
    baseline,
    table,
    kt_out,
    kp_out,
    res_out,
    one_lo,
    spread,
    left,
    right,
    part_send,
    part_recv,
    par_send,
    par_recv,
    img_send,
    img_recv,
    res_send,
    res_recv,
    full,
    part_sems,
    par_sems,
    img_sems,
    res_sems,
):
    _, coils, _, spokes, width = kspace.shape
    slab = owner.shape[1]
    rows = slab // width
    voxels = ktrans.shape[1]
    chunks = Chunks(width, voxels)
    height = chunks.height
    f = lax.axis_index("frames")
    j = lax.axis_index("coils")

    def peer(k):
        return lax.rem(f + k, n_frames)

    def coil_peer(k):
        return lax.rem(j + k, n_coils)

    barrier = pltpu.get_barrier_semaphore()

    def greet(k, _):
        pl.semaphore_signal(
            barrier, inc=1, device_id={"frames": peer(k), "coils": j}, device_id_type=MESH
        )
        return 0

    lax.fori_loop(1, n_frames, greet, 0)
    for k in range(1, n_coils):
        pl.semaphore_signal(
            barrier, inc=1, device_id={"frames": f, "coils": coil_peer(k)}, device_id_type=MESH
        )

    def exchange(send, recv, sems):
        def copy(k):
            to = peer(k)
            return pltpu.make_async_remote_copy(
                src_ref=send.at[to],
                dst_ref=recv.at[f],
                send_sem=sems.at[0, k],
                recv_sem=sems.at[1, k],
                device_id={"frames": to, "coils": j},
                device_id_type=MESH,
            )

        def arrival(k):
            source = lax.rem(f + n_frames - k, n_frames)
            return pltpu.make_async_remote_copy(
                src_ref=send.at[source],
                dst_ref=recv.at[source],
                send_sem=sems.at[0, k],
                recv_sem=sems.at[1, k],
                device_id={"frames": source, "coils": j},
                device_id_type=MESH,
            )

        def start():
            def body(k, _):
                copy(k).start()
                return 0

            lax.fori_loop(1, n_frames, body, 0)
            recv[f] = send[f]

        def wait():
            def body(k, _):
                arrival(k).wait_recv()
                return 0

            lax.fori_loop(1, n_frames, body, 0)

        def drain():
            def body(k, _):
                copy(k).wait_send()
                return 0

            lax.fori_loop(1, n_frames, body, 0)

        return start, wait, drain

    par_start, par_wait, par_drain = exchange(par_send, par_recv, par_sems)
    img_start, img_wait, img_drain = exchange(img_send, img_recv, img_sems)
    res_start, res_wait, res_drain = exchange(res_send, res_recv, res_sems)

    mine = pl.ds(pl.multiple_of(f * voxels, LANES), voxels)
    place = owner[0:1, mine]
    for c in range(1, n_coils):
        place = jnp.where(j == c, owner[c : c + 1, mine], place)
    lo = place & (width - 1)
    hi = lax.shift_right_logical(place, int(math.log2(width)))
    one_lo[...] = jnp.where(
        lax.broadcasted_iota(jnp.int32, (width, voxels), 0) == lo, 1.0, 0.0
    ).astype(BF16)
    in_row = lax.broadcasted_iota(jnp.int32, (rows, voxels), 0) == hi
    values = [ktrans[...], kep[...], baseline[0], baseline[1]]
    for p in range(4):
        spread[p * rows : (p + 1) * rows, :] = jnp.where(in_row, values[p], 0.0).astype(BF16)
    placed = lax.dot_general(spread[...], one_lo[...], NT, preferred_element_type=F32)
    for e in range(n_frames):
        pieces = []
        for p in range(4):
            pieces += chunks.take(placed[p * rows : (p + 1) * rows], e)
        par_send[e] = jnp.concatenate(pieces, 0).astype(BF16)
    pl.semaphore_wait(barrier, n_frames + n_coils - 2)
    par_start()

    number = spoke_index[...]
    turn = ((number * 40503) & 65535).astype(F32) * (2.0 * math.pi / 65536.0)
    live = jnp.where(
        lax.broadcasted_iota(jnp.int32, (1, spokes), 1) < count[0], 1.0, 0.0
    ).astype(F32)
    diagonal = lax.broadcasted_iota(jnp.int32, (spokes, spokes), 0) == (
        lax.broadcasted_iota(jnp.int32, (spokes, spokes), 1)
    )

    def column(row):
        return jnp.sum(jnp.where(diagonal, row, 0.0), 1, keepdims=True)

    w_cos = column(live * jnp.cos(turn))
    w_sin = column(live * jnp.sin(turn))
    first = column(offset[...].astype(F32)).astype(jnp.int32)
    tap = lax.broadcasted_iota(jnp.int32, (spokes, width), 1) - first
    band = jnp.where(
        (tap == 0) | (tap == 3), 0.25, jnp.where((tap == 1) | (tap == 2), 0.75, 0.0)
    )
    m_cos = band * w_cos
    m_sin = band * w_sin
    m_a = jnp.concatenate([m_cos, m_sin], 0).astype(BF16)
    m_b = jnp.concatenate([-m_sin, m_cos], 0).astype(BF16)
    left[...] = (
        lax.dot_general(table[:, :width], m_a, NT, preferred_element_type=F32)
        + lax.dot_general(table[:, width:], m_b, NT, preferred_element_type=F32)
    ).astype(BF16)

    lines = jnp.dot(
        kspace[0].reshape(coils * 2 * spokes, width), table[...], preferred_element_type=F32
    )
    for c in range(coils):
        real = lines[2 * c * spokes : (2 * c + 1) * spokes]
        imag = lines[(2 * c + 1) * spokes : (2 * c + 2) * spokes]
        h_r = (real[:, :width] - imag[:, width:]).astype(BF16)
        h_i = (real[:, width:] + imag[:, :width]).astype(BF16)
        at = 2 * c * width
        right[:spokes, at : at + width] = h_r
        right[:spokes, at + width : at + 2 * width] = h_i
        right[spokes:, at : at + width] = -h_i
        right[spokes:, at + width : at + 2 * width] = h_r

    def partial(which):
        top = pl.multiple_of(which * rows, rows)
        coil_image = jnp.dot(
            left[pl.ds(top, rows), :], right[...], preferred_element_type=F32
        )
        image_r = jnp.zeros((rows, width), F32)
        image_i = jnp.zeros((rows, width), F32)
        for c in range(coils):
            s_r = sens[c, 0, pl.ds(top, rows), :].astype(F32)
            s_i = sens[c, 1, pl.ds(top, rows), :].astype(F32)
            c_r = coil_image[:, 2 * c * width : (2 * c + 1) * width]
            c_i = coil_image[:, (2 * c + 1) * width : (2 * c + 2) * width]
            image_r = image_r + s_r * c_r + s_i * c_i
            image_i = image_i + s_r * c_i - s_i * c_r
        return image_r, image_i

    def part_copy(k):
        return pltpu.make_async_remote_copy(
            src_ref=part_send.at[k - 1],
            dst_ref=part_recv.at[k - 1],
            send_sem=part_sems.at[0, k],
            recv_sem=part_sems.at[1, k],
            device_id={"frames": f, "coils": coil_peer(k)},
            device_id_type=MESH,
        )

    for k in range(1, n_coils):
        image_r, image_i = partial(coil_peer(k))
        part_send[k - 1, 0] = image_r
        part_send[k - 1, 1] = image_i
        part_copy(k).start()
    image_r, image_i = partial(j)
    for k in range(1, n_coils):
        part_copy(k).wait_recv()
        image_r = image_r + part_recv[k - 1, 0]
        image_i = image_i + part_recv[k - 1, 1]
    for e in range(n_frames):
        pieces = chunks.take(image_r, e) + chunks.take(image_i, e)
        img_send[e] = jnp.concatenate(pieces, 0).astype(BF16)
    img_start()

    par_wait()
    params = par_recv[0].astype(F32)
    for e in range(1, n_frames):
        params = params + par_recv[e].astype(F32)
    kt, kp, base_r, base_i = [params[p * height : (p + 1) * height] for p in range(4)]
    taps = [aif[t] * STEP_MINUTES for t in range(n_frames)]
    decay = [jnp.exp(-(t * STEP_MINUTES) * kp) for t in range(n_frames)]
    drift = [decay[t] * -(t * STEP_MINUTES) for t in range(n_frames)]

    def convolve(curve, t):
        total = taps[t] * curve[0]
        for m in range(1, t + 1):
            total = total + taps[t - m] * curve[m]
        return total

    conc = [convolve(decay, t) for t in range(n_frames)]
    slope = [convolve(drift, t) for t in range(n_frames)]
    power = base_r * base_r + base_i * base_i
    h_aa = power * sum(c * c for c in conc)
    h_ab = power * kt * sum(c * s for c, s in zip(conc, slope))
    h_bb = power * kt * kt * sum(s * s for s in slope)
    d_aa = (1.0 + DAMPING) * h_aa + 1.0
    d_bb = (1.0 + DAMPING) * h_bb + 1.0
    determinant = d_aa * d_bb - h_ab * h_ab

    img_wait()
    g_a = jnp.zeros_like(kt)
    g_b = jnp.zeros_like(kt)
    for t in range(n_frames):
        image = img_recv[t].astype(F32)
        scale = 1.0 + kt * conc[t]
        project = base_r * (image[:height] - base_r * scale) + base_i * (
            image[height:] - base_i * scale
        )
        g_a = g_a + conc[t] * project
        g_b = g_b + slope[t] * project
    g_b = kt * g_b
    step_kt = (d_bb * g_a - h_ab * g_b) / determinant
    step_kp = (d_aa * g_b - h_ab * g_a) / determinant
    kt_next = kt + step_kt
    kp_next = kp + step_kp
    decay = [jnp.exp(-(t * STEP_MINUTES) * kp_next) for t in range(n_frames)]
    for t in range(n_frames):
        image = img_recv[t].astype(F32)
        scale = 1.0 + kt_next * convolve(decay, t)
        res_send[t] = jnp.concatenate(
            [image[:height] - base_r * scale, image[height:] - base_i * scale, step_kt, step_kp], 0
        ).astype(BF16)
    res_start()

    res_wait()
    for e in range(n_frames):
        block = res_recv[e].astype(F32)
        at = 0
        for p in range(4):
            for row, lanes in chunks.pieces(e):
                full[p * rows + row : p * rows + row + chunks.rows, lanes] = block[
                    at : at + chunks.rows
                ]
                at += chunks.rows
    for p in range(2):
        res_out[0, p] = full[p * rows : (p + 1) * rows, :].astype(BF16)
    picked = jnp.dot(
        full[2 * rows :, :].astype(BF16), one_lo[...], preferred_element_type=F32
    )
    in_row = lax.broadcasted_iota(jnp.int32, (rows, voxels), 0) == hi
    kt_out[...] = ktrans[...] + jnp.sum(
        jnp.where(in_row, picked[:rows], 0.0), 0, keepdims=True
    )
    kp_out[...] = kep[...] + jnp.sum(
        jnp.where(in_row, picked[rows:], 0.0), 0, keepdims=True
    )
    for k in range(1, n_coils):
        part_copy(k).wait_send()
    par_drain()
    img_drain()
    res_drain()


def shards(
    kspace,
    sensitivity,
    spoke_count,
    spoke_index,
    band_offset,
    owner_map,
    aif,
    ktrans,
    kep,
    baseline,
):
    n_frames = lax.axis_size("frames")
    n_coils = lax.axis_size("coils")
    _, coils, _, spokes, width = kspace.shape
    voxels = ktrans.shape[1]
    rows = owner_map.shape[1] // width
    height = voxels // LANES
    vmem = pl.BlockSpec(memory_space=pltpu.VMEM)
    smem = pl.BlockSpec(memory_space=pltpu.SMEM)
    pair = pltpu.SemaphoreType.DMA((2, n_frames))
    return pl.pallas_call(
        functools.partial(kernel, n_frames, n_coils),
        out_shape=[
            jax.ShapeDtypeStruct((1, voxels), F32),
            jax.ShapeDtypeStruct((1, voxels), F32),
            jax.ShapeDtypeStruct((1, 2, rows, width), BF16),
        ],
        in_specs=[vmem, vmem, smem, vmem, vmem, vmem, smem, vmem, vmem, vmem, vmem],
        out_specs=[vmem, vmem, vmem],
        scratch_shapes=[
            pltpu.VMEM((width, voxels), BF16),
            pltpu.VMEM((4 * rows, voxels), BF16),
            pltpu.VMEM((width, 2 * spokes), BF16),
            pltpu.VMEM((2 * spokes, coils * 2 * width), BF16),
            pltpu.VMEM((n_coils - 1, 2, rows, width), F32),
            pltpu.VMEM((n_coils - 1, 2, rows, width), F32),
            pltpu.VMEM((n_frames, 4 * height, LANES), BF16),
            pltpu.VMEM((n_frames, 4 * height, LANES), BF16),
            pltpu.VMEM((n_frames, 2 * height, LANES), BF16),
            pltpu.VMEM((n_frames, 2 * height, LANES), BF16),
            pltpu.VMEM((n_frames, 4 * height, LANES), BF16),
            pltpu.VMEM((n_frames, 4 * height, LANES), BF16),
            pltpu.VMEM((4 * rows, width), F32),
            pltpu.SemaphoreType.DMA((2, n_coils)),
            pair,
            pair,
            pair,
        ],
        compiler_params=pltpu.CompilerParams(
            collective_id=0, has_side_effects=True, vmem_limit_bytes=48 * 1024 * 1024
        ),
    )(
        kspace,
        sensitivity,
        spoke_count,
        spoke_index,
        band_offset,
        owner_map,
        aif,
        ktrans,
        kep,
        baseline.reshape(2, 1, voxels),
        dft_table(width),
    )


def solution(mesh):
    in_specs = (
        P("frames", "coils", None, None, None),
        P("coils", None, None, None),
        P("frames"),
        P("frames", None),
        P("frames", None),
        P(),
        P(),
        P("coils", "frames"),
        P("coils", "frames"),
        P(None, "coils", "frames"),
    )
    out_specs = (P("coils", "frames"), P("coils", "frames"), P("frames", None, "coils", None))
    return jax.shard_map(shards, mesh=mesh, in_specs=in_specs, out_specs=out_specs, check_vma=False)
```

time: 678 us -> 34.9 us (0.05)
  local copies, waits for them, and re-layouts: 420 us -> 8 us
  other arithmetic: 205 us -> 0 us
  Pallas kernels: 0 us -> 25.2 us
  waiting for transfers between devices: 16 us -> 0 us
  between operations: 15 us -> 1.38 us
  blocking collectives: 10.8 us -> 0 us
  starting transfers between devices: 6.81 us -> 0 us
    unnamed x1 -> x0, other arithmetic: 179 us -> none
    select_n x2 -> x0, local copies, waits for them, and re-layouts: 131 us -> none  [the longest x1 131 us: shards(): picked = jnp.take(slab, coil_row, axis=2)]
    gather x3 -> x0, local copies, waits for them, and re-layouts: 116 us -> none  [the longest x1 114 us: shards(): picked = jnp.take(slab, coil_row, axis=2)]
    scatter x1 -> x0, local copies, waits for them, and re-layouts: 86.5 us -> none  [shards(): placed = jnp.zeros_like(returned).at[:, :, coil_row].set(returned)]
    unnamed x24 -> x23, local copies, waits for them, and re-layouts: 44.5 us -> 8 us
    all_to_all x2 -> x0, local copies, waits for them, and re-layouts: 36.1 us -> none  [the longest x1 30.6 us: shards(): lax.all_to_all(picked, 'frames', split_axis=2, concat_axis=0, tiled=True)]
    pallas_call x0 -> x1, Pallas kernels: none -> 25.2 us  [shards(): pl.pallas_call(functools.partial(kernel, n_frames, n_coils), out_shape=[j...]
    select_n x3 -> x0, other arithmetic: 18.6 us -> none  [the longest x2 18.6 us: shards(): picked = jnp.take(slab, coil_row, axis=2)]
  transfers between devices with their start and end apart: 2 -> 0, of which waited for: 2 -> 0; matrix products, arithmetic and copies ran while one was open for 0% -> 0% of each run, Pallas kernels for 0% -> 0%
where the time goes in v1:
time: 34.9 us; the launch traced here: 34.5 us
  Pallas kernels  25.2 us (72%)
  local copies, waits for them, and re-layouts  8 us (23%)
  between operations  1.38 us (4%)
    pallas_call x1, Pallas kernels, shards(): pl.pallas_call(functools.partial(kernel, n_frames, n_coils), out_shape=[j...  25.2 us
    unnamed x23, local copies, waits for them, and re-layouts  8 us

profile of v1, /device:TPU:0, one launch (start us, length us, event | category | flops | bytes accessed | tf_op | source)
XLA Modules:
  0.0 34.5 jit_solution(6498055267725842415)
XLA Ops:
  0.6 0.0 copy-start.9
  0.6 0.0 copy-start.8
  0.7 0.0 copy-start.7
  1.3 0.0 copy-done.9
  1.3 0.0 copy-done.8
  1.4 0.0 copy-done.7
  1.4 0.0 copy-start
  1.4 1.2 %copy-done = bf16[4,2,256,256]{3,2,1,0:T(8,128)(2,1)S(1)} copy-done((bf16[4,2,256,256]{3,2,1,0:T(8,128)(2,1)S(1)}, bf16[4,2,256,256]{3,2,1,0:T(8,128)(2,1)}, u32[]{:S(2)}) %copy-start) | copy-done | bytes 1048600
  2.6 0.0 copy-start.1
  2.6 0.9 %copy-done.1 = s32[2,32768]{1,0:T(2,128)S(1)} copy-done((s32[2,32768]{1,0:T(2,128)S(1)}, s32[2,32768]{1,0:T(2,128)}, u32[]{:S(2)}) %copy-start.1) | copy-done | bytes 262168
  3.5 0.0 copy-start.2
  3.5 0.9 %copy-done.2 = bf16[256,512]{1,0:T(8,128)(2,1)S(1)} copy-done((bf16[256,512]{1,0:T(8,128)(2,1)S(1)}, bf16[256,512]{1,0:T(8,128)(2,1)}, u32[]{:S(2)}) %copy-start.2) | copy-done | bytes 262168
  4.5 0.0 copy-start.3
  4.5 0.9 %copy-done.3 = bf16[1,4,2,32,256]{4,3,2,1,0:T(8,128)(2,1)S(1)} copy-done((bf16[1,4,2,32,256]{4,3,2,1,0:T(8,128)(2,1)S(1)}, bf16[1,4,2,32,256]{4,3,2,1,0:T(8,128)(2,1)}, u32[]{:S(2)}) %copy-start.3) | copy-done | bytes 131096
  5.4 0.0 copy-start.4
  5.4 0.7 %copy-done.4 = f32[2,1,2048]{2,1,0:T(1,128)S(1)} copy-done((f32[2,1,2048]{2,1,0:T(1,128)S(1)}, f32[2,1,2048]{2,1,0:T(1,128)}, u32[]{:S(2)}) %copy-start.4) | copy-done | bytes 16408
  6.1 0.0 copy-start.5
  6.1 0.7 %copy-done.5 = f32[1,2048]{1,0:T(1,128)S(1)} copy-done((f32[1,2048]{1,0:T(1,128)S(1)}, f32[1,2048]{1,0:T(1,128)}, u32[]{:S(2)}) %copy-start.5) | copy-done | bytes 8216
  6.8 0.0 copy-start.6
  6.8 0.7 %copy-done.6 = f32[1,2048]{1,0:T(1,128)S(1)} copy-done((f32[1,2048]{1,0:T(1,128)S(1)}, f32[1,2048]{1,0:T(1,128)}, u32[]{:S(2)}) %copy-start.6) | copy-done | bytes 8216
  7.5 25.2 %shard_map.130 = (f32[1,2048]{1,0:T(1,128)S(1)}, f32[1,2048]{1,0:T(1,128)S(1)}, bf16[1,2,128,256]{3,2,1,0:T(8,128)(2,1)S(1)}) custom-call(bf16[1,4,2,32,256]{4,3,2,1,0:T(8,128)(2,1)S(1)} %copy-done.3, bf16[4,2,256,256]{3,2,1,0:T(8,128)(2,1)S(1)} %copy-done, s32[1]{0:T(128)S(6)} %copy.17.count, s32[1,32]{1,0:T(1,128)S(1)} %copy-done.7, ...), custom_call_target="tpu_custom_call" | custom-call | tf_op jit(solution)/shard_map/pallas_call | solution.py:365
  32.7 0.6 %copy.18 = f32[1,2048]{1,0:T(1,128)} copy(f32[1,2048]{1,0:T(1,128)S(1)} %get-tuple-element.6) | data formatting | bytes 16384
  33.3 0.6 %copy.19 = f32[1,2048]{1,0:T(1,128)} copy(f32[1,2048]{1,0:T(1,128)S(1)} %get-tuple-element.7) | data formatting | bytes 16384
  33.9 0.7 %copy.20 = bf16[1,2,128,256]{3,2,1,0:T(8,128)(2,1)} copy(bf16[1,2,128,256]{3,2,1,0:T(8,128)(2,1)S(1)} %get-tuple-element.8) | data formatting | bytes 262144
Async XLA Ops:
  0.6 0.7 %copy-start.9 = (f32[16]{0:T(128)S(1)}, f32[16]{0:T(128)}, u32[]{:S(2)}) copy-start(f32[16]{0:T(128)} %aif.1) | copy-start | bytes 196
  0.6 0.7 %copy-start.8 = (s32[1,32]{1,0:T(1,128)S(1)}, s32[1,32]{1,0:T(1,128)}, u32[]{:S(2)}) copy-start(s32[1,32]{1,0:T(1,128)} %offset.1) | copy-start | bytes 388
  0.7 0.7 %copy-start.7 = (s32[1,32]{1,0:T(1,128)S(1)}, s32[1,32]{1,0:T(1,128)}, u32[]{:S(2)}) copy-start(s32[1,32]{1,0:T(1,128)} %spoke_index.1) | copy-start | bytes 388
  1.4 1.2 %copy-start = (bf16[4,2,256,256]{3,2,1,0:T(8,128)(2,1)S(1)}, bf16[4,2,256,256]{3,2,1,0:T(8,128)(2,1)}, u32[]{:S(2)}) copy-start(bf16[4,2,256,256]{3,2,1,0:T(8,128)(2,1)} %sens.1) | copy-start | bytes 3145732
  2.6 0.9 %copy-start.1 = (s32[2,32768]{1,0:T(2,128)S(1)}, s32[2,32768]{1,0:T(2,128)}, u32[]{:S(2)}) copy-start(s32[2,32768]{1,0:T(2,128)} %owner.1) | copy-start | bytes 786436
  3.5 0.9 %copy-start.2 = (bf16[256,512]{1,0:T(8,128)(2,1)S(1)}, bf16[256,512]{1,0:T(8,128)(2,1)}, u32[]{:S(2)}) copy-start(bf16[256,512]{1,0:T(8,128)(2,1)} %constant.10.table) | copy-start | bytes 786436
  4.5 0.9 %copy-start.3 = (bf16[1,4,2,32,256]{4,3,2,1,0:T(8,128)(2,1)S(1)}, bf16[1,4,2,32,256]{4,3,2,1,0:T(8,128)(2,1)}, u32[]{:S(2)}) copy-start(bf16[1,4,2,32,256]{4,3,2,1,0:T(8,128)(2,1)} %kspace.1) | copy-start | bytes 393220
  5.4 0.7 %copy-start.4 = (f32[2,1,2048]{2,1,0:T(1,128)S(1)}, f32[2,1,2048]{2,1,0:T(1,128)}, u32[]{:S(2)}) copy-start(f32[2,1,2048]{2,1,0:T(1,128)} %baseline.1) | copy-start | bytes 49156
  6.1 0.7 %copy-start.5 = (f32[1,2048]{1,0:T(1,128)S(1)}, f32[1,2048]{1,0:T(1,128)}, u32[]{:S(2)}) copy-start(f32[1,2048]{1,0:T(1,128)} %ktrans.1) | copy-start | bytes 24580
  6.8 0.7 %copy-start.6 = (f32[1,2048]{1,0:T(1,128)S(1)}, f32[1,2048]{1,0:T(1,128)}, u32[]{:S(2)}) copy-start(f32[1,2048]{1,0:T(1,128)} %kep.1) | copy-start | bytes 24580

commit v2 on v1

--- a/solution.py
+++ b/solution.py
@@ -45,6 +45,20 @@
 def kernel(
     n_frames,
     n_coils,
+    kspace_in,
+    sens_in,
+    count_in,
+    spoke_index_in,
+    offset_in,
+    owner_in,
+    aif_in,
+    ktrans_in,
+    kep_in,
+    baseline_in,
+    table_in,
+    kt_out,
+    kp_out,
+    res_out,
     kspace,
     sens,
     count,
@@ -56,9 +70,7 @@
     kep,
     baseline,
     table,
-    kt_out,
-    kp_out,
-    res_out,
+    input_sems,
     one_lo,
     spread,
     left,
@@ -78,13 +90,33 @@
     res_sems,
 ):
     _, coils, _, spokes, width = kspace.shape
-    slab = owner.shape[1]
-    rows = slab // width
+    rows = owner_in.shape[1] // width
     voxels = ktrans.shape[1]
     chunks = Chunks(width, voxels)
     height = chunks.height
     f = lax.axis_index("frames")
     j = lax.axis_index("coils")
+    mine = pl.ds(pl.multiple_of(f * voxels, LANES), voxels)
+    loads = {}
+    for name, source, target in (
+        ("owner", owner_in.at[:, mine], owner),
+        ("ktrans", ktrans_in, ktrans),
+        ("kep", kep_in, kep),
+        ("baseline", baseline_in, baseline),
+        ("table", table_in, table),
+        ("index", spoke_index_in, spoke_index),
+        ("offset", offset_in, offset),
+        ("count", count_in, count),
+        ("kspace", kspace_in, kspace),
+        ("sens", sens_in, sens),
+        ("aif", aif_in, aif),
+    ):
+        loads[name] = pltpu.make_async_copy(source, target, input_sems.at[len(loads)])
+        loads[name].start()
+
+    def loaded(*names):
+        for name in names:
+            loads[name].wait()
 
     def peer(k):
         return lax.rem(f + k, n_frames)
@@ -157,10 +189,10 @@
     img_start, img_wait, img_drain = exchange(img_send, img_recv, img_sems)
     res_start, res_wait, res_drain = exchange(res_send, res_recv, res_sems)
 
-    mine = pl.ds(pl.multiple_of(f * voxels, LANES), voxels)
-    place = owner[0:1, mine]
+    loaded("owner", "ktrans", "kep", "baseline")
+    place = owner[0:1, :]
     for c in range(1, n_coils):
-        place = jnp.where(j == c, owner[c : c + 1, mine], place)
+        place = jnp.where(j == c, owner[c : c + 1, :], place)
     lo = place & (width - 1)
     hi = lax.shift_right_logical(place, int(math.log2(width)))
     one_lo[...] = jnp.where(
@@ -179,6 +211,7 @@
     pl.semaphore_wait(barrier, n_frames + n_coils - 2)
     par_start()
 
+    loaded("index", "offset", "count", "table")
     number = spoke_index[...]
     turn = ((number * 40503) & 65535).astype(F32) * (2.0 * math.pi / 65536.0)
     live = jnp.where(
@@ -207,6 +240,7 @@
         + lax.dot_general(table[:, width:], m_b, NT, preferred_element_type=F32)
     ).astype(BF16)
 
+    loaded("kspace")
     lines = jnp.dot(
         kspace[0].reshape(coils * 2 * spokes, width), table[...], preferred_element_type=F32
     )
@@ -237,6 +271,8 @@
             image_i = image_i + s_r * c_i - s_i * c_r
         return image_r, image_i
 
+    loaded("sens")
+
     def part_copy(k):
         return pltpu.make_async_remote_copy(
             src_ref=part_send.at[k - 1],
@@ -267,6 +303,7 @@
     for e in range(1, n_frames):
         params = params + par_recv[e].astype(F32)
     kt, kp, base_r, base_i = [params[p * height : (p + 1) * height] for p in range(4)]
+    loaded("aif")
     taps = [aif[t] * STEP_MINUTES for t in range(n_frames)]
     decay = [jnp.exp(-(t * STEP_MINUTES) * kp) for t in range(n_frames)]
     drift = [decay[t] * -(t * STEP_MINUTES) for t in range(n_frames)]
@@ -360,7 +397,24 @@
     rows = owner_map.shape[1] // width
     height = voxels // LANES
     vmem = pl.BlockSpec(memory_space=pltpu.VMEM)
-    smem = pl.BlockSpec(memory_space=pltpu.SMEM)
+    hbm = pl.BlockSpec(memory_space=pltpu.HBM)
+    operands = (
+        kspace,
+        sensitivity,
+        spoke_count,
+        spoke_index,
+        band_offset,
+        owner_map,
+        aif,
+        ktrans,
+        kep,
+        baseline.reshape(2, 1, voxels),
+        dft_table(width),
+    )
+    landing = [
+        (pltpu.SMEM if x.ndim == 1 else pltpu.VMEM)(x.shape, x.dtype) for x in operands
+    ]
+    landing[5] = pltpu.VMEM((n_coils, voxels), jnp.int32)
     pair = pltpu.SemaphoreType.DMA((2, n_frames))
     return pl.pallas_call(
         functools.partial(kernel, n_frames, n_coils),
@@ -369,9 +423,11 @@
             jax.ShapeDtypeStruct((1, voxels), F32),
             jax.ShapeDtypeStruct((1, 2, rows, width), BF16),
         ],
-        in_specs=[vmem, vmem, smem, vmem, vmem, vmem, smem, vmem, vmem, vmem, vmem],
+        in_specs=[hbm] * len(operands),
         out_specs=[vmem, vmem, vmem],
-        scratch_shapes=[
+        scratch_shapes=landing
+        + [
+            pltpu.SemaphoreType.DMA((len(operands),)),
             pltpu.VMEM((width, voxels), BF16),
             pltpu.VMEM((4 * rows, voxels), BF16),
             pltpu.VMEM((width, 2 * spokes), BF16),
@@ -391,21 +447,9 @@
             pair,
         ],
         compiler_params=pltpu.CompilerParams(
-            collective_id=0, has_side_effects=True, vmem_limit_bytes=48 * 1024 * 1024
+            collective_id=0, has_side_effects=True, vmem_limit_bytes=56 * 1024 * 1024
         ),
-    )(
-        kspace,
-        sensitivity,
-        spoke_count,
-        spoke_index,
-        band_offset,
-        owner_map,
-        aif,
-        ktrans,
-        kep,
-        baseline.reshape(2, 1, voxels),
-        dft_table(width),
-    )
+    )(*operands)
 
 
 def solution(mesh):

time: 34.9 us -> 30.4 us (0.87)
  local copies, waits for them, and re-layouts: 8 us -> 3.47 us
    unnamed x23 -> x5, local copies, waits for them, and re-layouts: 8 us -> 3.47 us
where the time goes in v2:
time: 30.4 us; the launch traced here: 30.1 us
  Pallas kernels  25.3 us (83%)
  local copies, waits for them, and re-layouts  3.47 us (11%)
  between operations  1.3 us (4%)
    pallas_call x1, Pallas kernels, shards(): pl.pallas_call(functools.partial(kernel, n_frames, n_coils), out_shape=[j...  25.3 us
    unnamed x5, local copies, waits for them, and re-layouts  3.47 us

profile of v2, /device:TPU:0, one launch (start us, length us, event | category | flops | bytes accessed | tf_op | source)
XLA Modules:
  0.0 30.1 jit_solution(9252726622489774689)
XLA Ops:
  1.3 25.3 %shard_map.130 = (f32[1,2048]{1,0:T(1,128)}, f32[1,2048]{1,0:T(1,128)}, bf16[1,2,128,256]{3,2,1,0:T(8,128)(2,1)}) custom-call(bf16[1,4,2,32,256]{4,3,2,1,0:T(8,128)(2,1)} %kspace_in.1, bf16[4,2,256,256]{3,2,1,0:T(8,128)(2,1)} %sens_in.1, s32[1]{0:T(128)S(6)} %copy.17.count_in, s32[1,32]{1,0:T(1,128)} %spoke_index_in.1, s32[1,32]{1,0:T(1,128)} %offset_in.1, ...), custom_call_target="tpu_custom_call" | custom-call | tf_op jit(solution)/shard_map/pallas_call | solution.py:419
  26.6 0.0 copy-start
  26.6 1.3 %copy.18 = f32[1,2048]{1,0:T(1,128)} copy(f32[1,2048]{1,0:T(1,128)} %get-tuple-element.6) | data formatting | bytes 16384
  27.9 0.0 copy-done
  27.9 0.6 %copy.19 = f32[1,2048]{1,0:T(1,128)} copy(f32[1,2048]{1,0:T(1,128)S(1)} %copy-done) | data formatting | bytes 16384
  28.5 1.6 %copy.20 = bf16[1,2,128,256]{3,2,1,0:T(8,128)(2,1)} copy(bf16[1,2,128,256]{3,2,1,0:T(8,128)(2,1)} %get-tuple-element.8) | data formatting | bytes 262144
Async XLA Ops:
  26.6 1.3 %copy-start = (f32[1,2048]{1,0:T(1,128)S(1)}, f32[1,2048]{1,0:T(1,128)}, u32[]{:S(2)}) copy-start(f32[1,2048]{1,0:T(1,128)} %get-tuple-element.7) | copy-start | bytes 24580

commit v3 on v2

--- a/solution.py
+++ b/solution.py
@@ -208,8 +208,6 @@
         for p in range(4):
             pieces += chunks.take(placed[p * rows : (p + 1) * rows], e)
         par_send[e] = jnp.concatenate(pieces, 0).astype(BF16)
-    pl.semaphore_wait(barrier, n_frames + n_coils - 2)
-    par_start()
 
     loaded("index", "offset", "count", "table")
     number = spoke_index[...]
@@ -287,7 +285,10 @@
         image_r, image_i = partial(coil_peer(k))
         part_send[k - 1, 0] = image_r
         part_send[k - 1, 1] = image_i
+    pl.semaphore_wait(barrier, n_frames + n_coils - 2)
+    for k in range(1, n_coils):
         part_copy(k).start()
+    par_start()
     image_r, image_i = partial(j)
     for k in range(1, n_coils):
         part_copy(k).wait_recv()
@@ -376,6 +377,18 @@
     par_drain()
     img_drain()
     res_drain()
+
+
+def hand_over(*refs):
+    count = (len(refs) - 1) // 2
+    sems = refs[-1]
+    copies = [
+        pltpu.make_async_copy(refs[i], refs[count + i], sems.at[i]) for i in range(count)
+    ]
+    for copy in copies:
+        copy.start()
+    for copy in copies:
+        copy.wait()
 
 
 def shards(
@@ -416,7 +429,7 @@
     ]
     landing[5] = pltpu.VMEM((n_coils, voxels), jnp.int32)
     pair = pltpu.SemaphoreType.DMA((2, n_frames))
-    return pl.pallas_call(
+    results = pl.pallas_call(
         functools.partial(kernel, n_frames, n_coils),
         out_shape=[
             jax.ShapeDtypeStruct((1, voxels), F32),
@@ -450,6 +463,14 @@
             collective_id=0, has_side_effects=True, vmem_limit_bytes=56 * 1024 * 1024
         ),
     )(*operands)
+    return pl.pallas_call(
+        hand_over,
+        out_shape=[jax.ShapeDtypeStruct(x.shape, x.dtype) for x in results],
+        in_specs=[hbm] * len(results),
+        out_specs=[hbm] * len(results),
+        scratch_shapes=[pltpu.SemaphoreType.DMA((len(results),))],
+        compiler_params=pltpu.CompilerParams(vmem_limit_bytes=56 * 1024 * 1024),
+    )(*results)
 
 
 def solution(mesh):

time: 30.4 us -> 32.5 us (1.069)
  Pallas kernels: 25.3 us -> 30.9 us
  local copies, waits for them, and re-layouts: 3.47 us -> 0 us
    pallas_call x0 -> x1, Pallas kernels: none -> 5.6 us  [shards(): pl.pallas_call(hand_over, out_shape=[jax.ShapeDtypeStruct(x.shape, x.dtyp...]
    unnamed x5 -> x0, local copies, waits for them, and re-layouts: 3.47 us -> none
where the time goes in v3:
time: 32.5 us; the launch traced here: 32.2 us
  Pallas kernels  30.9 us (95%)
  between operations  1.29 us (4%)
    pallas_call x1, Pallas kernels, shards(): pl.pallas_call(functools.partial(kernel, n_frames, n_coils), out_shape=[j...  25.3 us
    pallas_call x1, Pallas kernels, shards(): pl.pallas_call(hand_over, out_shape=[jax.ShapeDtypeStruct(x.shape, x.dtyp...  5.6 us

profile of v3, /device:TPU:0, one launch (start us, length us, event | category | flops | bytes accessed | tf_op | source)
XLA Modules:
  0.0 32.2 jit_solution(9061338302055727039)
XLA Ops:
  1.3 25.3 %shard_map.130 = (f32[1,2048]{1,0:T(1,128)}, f32[1,2048]{1,0:T(1,128)}, bf16[1,2,128,256]{3,2,1,0:T(8,128)(2,1)}) custom-call(bf16[1,4,2,32,256]{4,3,2,1,0:T(8,128)(2,1)} %kspace_in.1, bf16[4,2,256,256]{3,2,1,0:T(8,128)(2,1)} %sens_in.1, s32[1]{0:T(128)S(6)} %copy.14.count_in, s32[1,32]{1,0:T(1,128)} %spoke_index_in.1, s32[1,32]{1,0:T(1,128)} %offset_in.1, ...), custom_call_target="tpu_custom_call" | custom-call | tf_op jit(solution)/shard_map/pallas_call | solution.py:432
  26.6 5.6 %shard_map.131 = (f32[1,2048]{1,0:T(1,128)}, f32[1,2048]{1,0:T(1,128)}, bf16[1,2,128,256]{3,2,1,0:T(8,128)(2,1)}) custom-call(f32[1,2048]{1,0:T(1,128)} %get-tuple-element.6.refs_0_, f32[1,2048]{1,0:T(1,128)} %get-tuple-element.7.refs_1_, bf16[1,2,128,256]{3,2,1,0:T(8,128)(2,1)} %get-tuple-element.8.refs_2_), custom_call_target="tpu_custom_call" | custom-call | tf_op jit(solution)/shard_map/pallas_call | solution.py:466

commit v4 on v3

--- a/solution.py
+++ b/solution.py
@@ -71,6 +71,9 @@
     baseline,
     table,
     input_sems,
+    raw_rows,
+    raw_send,
+    raw_recv,
     one_lo,
     spread,
     left,
@@ -81,13 +84,22 @@
     par_recv,
     img_send,
     img_recv,
+    step_send,
+    step_recv,
     res_send,
     res_recv,
+    steps,
+    pick_rows,
+    pick_send,
+    pick_recv,
     full,
     part_sems,
+    raw_sems,
     par_sems,
     img_sems,
+    step_sems,
     res_sems,
+    pick_sems,
 ):
     _, coils, _, spokes, width = kspace.shape
     rows = owner_in.shape[1] // width
@@ -96,10 +108,16 @@
     height = chunks.height
     f = lax.axis_index("frames")
     j = lax.axis_index("coils")
-    mine = pl.ds(pl.multiple_of(f * voxels, LANES), voxels)
+    n_lines, n_plane = raw_recv.shape[0], par_recv.shape[0]
+    plane_rows = rows // n_lines
+    z, q = f // n_plane, lax.rem(f, n_plane)
+
+    def slots(number):
+        start = (number * n_plane + q) * voxels
+        return pl.ds(pl.multiple_of(start, LANES), voxels)
+
     loads = {}
     for name, source, target in (
-        ("owner", owner_in.at[:, mine], owner),
         ("ktrans", ktrans_in, ktrans),
         ("kep", kep_in, kep),
         ("baseline", baseline_in, baseline),
@@ -110,6 +128,10 @@
         ("kspace", kspace_in, kspace),
         ("sens", sens_in, sens),
         ("aif", aif_in, aif),
+        *[
+            (b, owner_in.at[:, slots(b)], owner.at[:, b * voxels : (b + 1) * voxels])
+            for b in range(n_lines)
+        ],
     ):
         loads[name] = pltpu.make_async_copy(source, target, input_sems.at[len(loads)])
         loads[name].start()
@@ -138,76 +160,63 @@
             barrier, inc=1, device_id={"frames": f, "coils": coil_peer(k)}, device_id_type=MESH
         )
 
-    def exchange(send, recv, sems):
-        def copy(k):
-            to = peer(k)
+    def exchange(send, recv, sems, size, me, device, split):
+        def block(number):
+            return send.at[number] if split else send
+
+        def copy(k, to, slot):
             return pltpu.make_async_remote_copy(
-                src_ref=send.at[to],
-                dst_ref=recv.at[f],
+                src_ref=block(to),
+                dst_ref=recv.at[slot],
                 send_sem=sems.at[0, k],
                 recv_sem=sems.at[1, k],
-                device_id={"frames": to, "coils": j},
+                device_id={"frames": device(to), "coils": j},
                 device_id_type=MESH,
             )
 
-        def arrival(k):
-            source = lax.rem(f + n_frames - k, n_frames)
-            return pltpu.make_async_remote_copy(
-                src_ref=send.at[source],
-                dst_ref=recv.at[source],
-                send_sem=sems.at[0, k],
-                recv_sem=sems.at[1, k],
-                device_id={"frames": source, "coils": j},
-                device_id_type=MESH,
-            )
-
         def start():
             def body(k, _):
-                copy(k).start()
+                copy(k, lax.rem(me + k, size), me).start()
                 return 0
 
-            lax.fori_loop(1, n_frames, body, 0)
-            recv[f] = send[f]
+            lax.fori_loop(1, size, body, 0)
+            recv[me] = send[me] if split else send[...]
 
         def wait():
             def body(k, _):
-                arrival(k).wait_recv()
+                source = lax.rem(me + size - k, size)
+                copy(k, source, source).wait_recv()
                 return 0
 
-            lax.fori_loop(1, n_frames, body, 0)
+            lax.fori_loop(1, size, body, 0)
 
         def drain():
             def body(k, _):
-                copy(k).wait_send()
+                copy(k, lax.rem(me + k, size), me).wait_send()
                 return 0
 
-            lax.fori_loop(1, n_frames, body, 0)
+            lax.fori_loop(1, size, body, 0)
 
         return start, wait, drain
 
-    par_start, par_wait, par_drain = exchange(par_send, par_recv, par_sems)
-    img_start, img_wait, img_drain = exchange(img_send, img_recv, img_sems)
-    res_start, res_wait, res_drain = exchange(res_send, res_recv, res_sems)
-
-    loaded("owner", "ktrans", "kep", "baseline")
-    place = owner[0:1, :]
-    for c in range(1, n_coils):
-        place = jnp.where(j == c, owner[c : c + 1, :], place)
-    lo = place & (width - 1)
-    hi = lax.shift_right_logical(place, int(math.log2(width)))
-    one_lo[...] = jnp.where(
-        lax.broadcasted_iota(jnp.int32, (width, voxels), 0) == lo, 1.0, 0.0
-    ).astype(BF16)
-    in_row = lax.broadcasted_iota(jnp.int32, (rows, voxels), 0) == hi
-    values = [ktrans[...], kep[...], baseline[0], baseline[1]]
-    for p in range(4):
-        spread[p * rows : (p + 1) * rows, :] = jnp.where(in_row, values[p], 0.0).astype(BF16)
-    placed = lax.dot_general(spread[...], one_lo[...], NT, preferred_element_type=F32)
-    for e in range(n_frames):
-        pieces = []
-        for p in range(4):
-            pieces += chunks.take(placed[p * rows : (p + 1) * rows], e)
-        par_send[e] = jnp.concatenate(pieces, 0).astype(BF16)
+    line = (n_lines, z, lambda number: number * n_plane + q)
+    plane = (n_plane, q, lambda number: z * n_plane + number)
+    everyone = (n_frames, f, lambda number: number)
+    raw_start, raw_wait, raw_drain = exchange(raw_send, raw_recv, raw_sems, *line, False)
+    par_start, par_wait, par_drain = exchange(par_send, par_recv, par_sems, *plane, True)
+    img_start, img_wait, img_drain = exchange(img_send, img_recv, img_sems, *everyone, True)
+    res_start, res_wait, res_drain = exchange(res_send, res_recv, res_sems, *everyone, True)
+    step_start, step_wait, step_drain = exchange(step_send, step_recv, step_sems, *plane, False)
+    pick_start, pick_wait, pick_drain = exchange(pick_send, pick_recv, pick_sems, *line, True)
+
+    loaded("ktrans", "kep", "baseline")
+    folds, fold = raw_rows.shape[0] // 4, raw_rows.shape[1]
+    for p, value in enumerate((ktrans[...], kep[...], baseline[0], baseline[1])):
+        for i in range(folds):
+            raw_rows[p * folds + i : p * folds + i + 1, :] = value[:, i * fold : (i + 1) * fold]
+    raw_send[...] = raw_rows[...].astype(BF16)
+    pl.semaphore_wait(barrier, n_frames + n_coils - 2)
+    raw_start()
 
     loaded("index", "offset", "count", "table")
     number = spoke_index[...]
@@ -285,10 +294,40 @@
         image_r, image_i = partial(coil_peer(k))
         part_send[k - 1, 0] = image_r
         part_send[k - 1, 1] = image_i
-    pl.semaphore_wait(barrier, n_frames + n_coils - 2)
-    for k in range(1, n_coils):
         part_copy(k).start()
+
+    loaded(*range(n_lines))
+    place = owner[0:1, :]
+    for c in range(1, n_coils):
+        place = jnp.where(j == c, owner[c : c + 1, :], place)
+    lo = place & (width - 1)
+    hi = lax.shift_right_logical(place, int(math.log2(width))) - z * plane_rows
+    for b in range(n_lines):
+        cut = slice(b * voxels, (b + 1) * voxels)
+        one_lo[:, cut] = jnp.where(
+            lax.broadcasted_iota(jnp.int32, (width, voxels), 0) == lo[:, cut], 1.0, 0.0
+        ).astype(BF16)
+    raw_wait()
+    for b in range(n_lines):
+        block = raw_recv[b].astype(F32)
+        for i in range(folds):
+            cut = slice(b * voxels + i * fold, b * voxels + (i + 1) * fold)
+            in_row = lax.broadcasted_iota(jnp.int32, (plane_rows, fold), 0) == hi[:, cut]
+            spread[:, cut] = jnp.concatenate(
+                [
+                    jnp.where(in_row, block[p * folds + i : p * folds + i + 1], 0.0)
+                    for p in range(4)
+                ],
+                0,
+            ).astype(BF16)
+    placed = lax.dot_general(spread[...], one_lo[...], NT, preferred_element_type=F32)
+    for e in range(n_plane):
+        pieces = []
+        for p in range(4):
+            pieces += chunks.take(placed[p * plane_rows : (p + 1) * plane_rows], e)
+        par_send[e] = jnp.concatenate(pieces, 0).astype(BF16)
     par_start()
+
     image_r, image_i = partial(j)
     for k in range(1, n_coils):
         part_copy(k).wait_recv()
@@ -301,7 +340,7 @@
 
     par_wait()
     params = par_recv[0].astype(F32)
-    for e in range(1, n_frames):
+    for e in range(1, n_plane):
         params = params + par_recv[e].astype(F32)
     kt, kp, base_r, base_i = [params[p * height : (p + 1) * height] for p in range(4)]
     loaded("aif")
@@ -339,6 +378,8 @@
     g_b = kt * g_b
     step_kt = (d_bb * g_a - h_ab * g_b) / determinant
     step_kp = (d_aa * g_b - h_ab * g_a) / determinant
+    step_send[...] = jnp.concatenate([step_kt, step_kp], 0).astype(BF16)
+    step_start()
     kt_next = kt + step_kt
     kp_next = kp + step_kp
     decay = [jnp.exp(-(t * STEP_MINUTES) * kp_next) for t in range(n_frames)]
@@ -346,48 +387,79 @@
         image = img_recv[t].astype(F32)
         scale = 1.0 + kt_next * convolve(decay, t)
         res_send[t] = jnp.concatenate(
-            [image[:height] - base_r * scale, image[height:] - base_i * scale, step_kt, step_kp], 0
+            [image[:height] - base_r * scale, image[height:] - base_i * scale], 0
         ).astype(BF16)
     res_start()
 
+    def unpack(block, target, stride, number, planes):
+        at = 0
+        for p in range(planes):
+            for row, lanes in chunks.pieces(number):
+                top = p * stride + row
+                target[top : top + chunks.rows, lanes] = block[at : at + chunks.rows]
+                at += chunks.rows
+
+    step_wait()
+    for e in range(n_plane):
+        unpack(step_recv[e].astype(F32), steps, plane_rows, e, 2)
+    pick_folds, pick_fold = pick_rows.shape[0] // 2, pick_rows.shape[1]
+    for b in range(n_lines):
+        cut = slice(b * voxels, (b + 1) * voxels)
+        picked = jnp.dot(
+            steps[...].astype(BF16), one_lo[:, cut], preferred_element_type=F32
+        )
+        in_row = lax.broadcasted_iota(jnp.int32, (plane_rows, voxels), 0) == hi[:, cut]
+        for p in range(2):
+            chosen = jnp.sum(
+                jnp.where(in_row, picked[p * plane_rows : (p + 1) * plane_rows], 0.0),
+                0,
+                keepdims=True,
+            )
+            for i in range(pick_folds):
+                pick_rows[p * pick_folds + i : p * pick_folds + i + 1, :] = chosen[
+                    :, i * pick_fold : (i + 1) * pick_fold
+                ]
+        pick_send[b] = pick_rows[...].astype(BF16)
+    pick_start()
+
     res_wait()
     for e in range(n_frames):
-        block = res_recv[e].astype(F32)
-        at = 0
-        for p in range(4):
-            for row, lanes in chunks.pieces(e):
-                full[p * rows + row : p * rows + row + chunks.rows, lanes] = block[
-                    at : at + chunks.rows
-                ]
-                at += chunks.rows
+        unpack(res_recv[e].astype(F32), full, rows, e, 2)
     for p in range(2):
         res_out[0, p] = full[p * rows : (p + 1) * rows, :].astype(BF16)
-    picked = jnp.dot(
-        full[2 * rows :, :].astype(BF16), one_lo[...], preferred_element_type=F32
-    )
-    in_row = lax.broadcasted_iota(jnp.int32, (rows, voxels), 0) == hi
-    kt_out[...] = ktrans[...] + jnp.sum(
-        jnp.where(in_row, picked[:rows], 0.0), 0, keepdims=True
-    )
-    kp_out[...] = kep[...] + jnp.sum(
-        jnp.where(in_row, picked[rows:], 0.0), 0, keepdims=True
-    )
+    pick_wait()
+    total = pick_recv[0].astype(F32)
+    for b in range(1, n_lines):
+        total = total + pick_recv[b].astype(F32)
+    for p, (old, new) in enumerate(((ktrans, kt_out), (kep, kp_out))):
+        for i in range(pick_folds):
+            cut = slice(i * pick_fold, (i + 1) * pick_fold)
+            row = p * pick_folds + i
+            new[:, cut] = old[:, cut] + total[row : row + 1]
     for k in range(1, n_coils):
         part_copy(k).wait_send()
+    raw_drain()
     par_drain()
     img_drain()
+    step_drain()
     res_drain()
+    pick_drain()
 
 
 def hand_over(*refs):
-    count = (len(refs) - 1) // 2
+    count = len(refs) // 3
     sems = refs[-1]
-    copies = [
-        pltpu.make_async_copy(refs[i], refs[count + i], sems.at[i]) for i in range(count)
-    ]
-    for copy in copies:
+    into, out = [], []
+    for i in range(count):
+        held = refs[2 * count + i]
+        into.append(pltpu.make_async_copy(refs[i], held, sems.at[0, i]))
+        out.append(pltpu.make_async_copy(held, refs[count + i], sems.at[1, i]))
+    for copy in into:
         copy.start()
-    for copy in copies:
+    for i in range(count):
+        into[i].wait()
+        out[i].start()
+    for copy in out:
         copy.wait()
 
 
@@ -409,6 +481,13 @@
     voxels = ktrans.shape[1]
     rows = owner_map.shape[1] // width
     height = voxels // LANES
+    n_plane = 1
+    while n_plane * n_plane < n_frames:
+        n_plane *= 2
+    n_lines = n_frames // n_plane
+    plane_rows = rows // n_lines
+    folds = 4 if voxels % (4 * LANES) == 0 else 1
+    pick_folds = 8 if voxels % (8 * LANES) == 0 else 1
     vmem = pl.BlockSpec(memory_space=pltpu.VMEM)
     hbm = pl.BlockSpec(memory_space=pltpu.HBM)
     operands = (
@@ -427,8 +506,7 @@
     landing = [
         (pltpu.SMEM if x.ndim == 1 else pltpu.VMEM)(x.shape, x.dtype) for x in operands
     ]
-    landing[5] = pltpu.VMEM((n_coils, voxels), jnp.int32)
-    pair = pltpu.SemaphoreType.DMA((2, n_frames))
+    landing[5] = pltpu.VMEM((n_coils, n_lines * voxels), jnp.int32)
     results = pl.pallas_call(
         functools.partial(kernel, n_frames, n_coils),
         out_shape=[
@@ -440,24 +518,36 @@
         out_specs=[vmem, vmem, vmem],
         scratch_shapes=landing
         + [
-            pltpu.SemaphoreType.DMA((len(operands),)),
-            pltpu.VMEM((width, voxels), BF16),
-            pltpu.VMEM((4 * rows, voxels), BF16),
+            pltpu.SemaphoreType.DMA((len(operands) - 1 + n_lines,)),
+            pltpu.VMEM((4 * folds, voxels // folds), F32),
+            pltpu.VMEM((4 * folds, voxels // folds), BF16),
+            pltpu.VMEM((n_lines, 4 * folds, voxels // folds), BF16),
+            pltpu.VMEM((width, n_lines * voxels), BF16),
+            pltpu.VMEM((4 * plane_rows, n_lines * voxels), BF16),
             pltpu.VMEM((width, 2 * spokes), BF16),
             pltpu.VMEM((2 * spokes, coils * 2 * width), BF16),
             pltpu.VMEM((n_coils - 1, 2, rows, width), F32),
             pltpu.VMEM((n_coils - 1, 2, rows, width), F32),
-            pltpu.VMEM((n_frames, 4 * height, LANES), BF16),
-            pltpu.VMEM((n_frames, 4 * height, LANES), BF16),
+            pltpu.VMEM((n_plane, 4 * height, LANES), BF16),
+            pltpu.VMEM((n_plane, 4 * height, LANES), BF16),
             pltpu.VMEM((n_frames, 2 * height, LANES), BF16),
             pltpu.VMEM((n_frames, 2 * height, LANES), BF16),
-            pltpu.VMEM((n_frames, 4 * height, LANES), BF16),
-            pltpu.VMEM((n_frames, 4 * height, LANES), BF16),
-            pltpu.VMEM((4 * rows, width), F32),
+            pltpu.VMEM((2 * height, LANES), BF16),
+            pltpu.VMEM((n_plane, 2 * height, LANES), BF16),
+            pltpu.VMEM((n_frames, 2 * height, LANES), BF16),
+            pltpu.VMEM((n_frames, 2 * height, LANES), BF16),
+            pltpu.VMEM((2 * plane_rows, width), F32),
+            pltpu.VMEM((2 * pick_folds, voxels // pick_folds), F32),
+            pltpu.VMEM((n_lines, 2 * pick_folds, voxels // pick_folds), BF16),
+            pltpu.VMEM((n_lines, 2 * pick_folds, voxels // pick_folds), BF16),
+            pltpu.VMEM((2 * rows, width), F32),
             pltpu.SemaphoreType.DMA((2, n_coils)),
-            pair,
-            pair,
-            pair,
+            pltpu.SemaphoreType.DMA((2, n_lines)),
+            pltpu.SemaphoreType.DMA((2, n_plane)),
+            pltpu.SemaphoreType.DMA((2, n_frames)),
+            pltpu.SemaphoreType.DMA((2, n_plane)),
+            pltpu.SemaphoreType.DMA((2, n_frames)),
+            pltpu.SemaphoreType.DMA((2, n_lines)),
         ],
         compiler_params=pltpu.CompilerParams(
             collective_id=0, has_side_effects=True, vmem_limit_bytes=56 * 1024 * 1024
@@ -468,7 +558,8 @@
         out_shape=[jax.ShapeDtypeStruct(x.shape, x.dtype) for x in results],
         in_specs=[hbm] * len(results),
         out_specs=[hbm] * len(results),
-        scratch_shapes=[pltpu.SemaphoreType.DMA((len(results),))],
+        scratch_shapes=[pltpu.VMEM(x.shape, x.dtype) for x in results]
+        + [pltpu.SemaphoreType.DMA((2, len(results)))],
         compiler_params=pltpu.CompilerParams(vmem_limit_bytes=56 * 1024 * 1024),
     )(*results)
 

time: 32.5 us -> 31.5 us (0.969)
  Pallas kernels: 30.9 us -> 30 us
    pallas_call x1, Pallas kernels: 5.6 us -> 1.65 us  [shards(): pl.pallas_call(hand_over, out_shape=[jax.ShapeDtypeStruct(x.shape, x.dtyp...]
    pallas_call x1, Pallas kernels: 25.3 us -> 28.3 us  [shards(): pl.pallas_call(functools.partial(kernel, n_frames, n_coils), out_shape=[j...]
where the time goes in v4:
time: 31.5 us; the launch traced here: 31.2 us
  Pallas kernels  30 us (95%)
  between operations  1.29 us (4%)
    pallas_call x1, Pallas kernels, shards(): pl.pallas_call(functools.partial(kernel, n_frames, n_coils), out_shape=[j...  28.3 us
    pallas_call x1, Pallas kernels, shards(): pl.pallas_call(hand_over, out_shape=[jax.ShapeDtypeStruct(x.shape, x.dtyp...  1.65 us

profile of v4, /device:TPU:0, one launch (start us, length us, event | category | flops | bytes accessed | tf_op | source)
XLA Modules:
  0.0 31.2 jit_solution(14284048288831200672)
XLA Ops:
  1.3 28.3 %shard_map.130 = (f32[1,2048]{1,0:T(1,128)}, f32[1,2048]{1,0:T(1,128)}, bf16[1,2,128,256]{3,2,1,0:T(8,128)(2,1)}) custom-call(bf16[1,4,2,32,256]{4,3,2,1,0:T(8,128)(2,1)} %kspace_in.1, bf16[4,2,256,256]{3,2,1,0:T(8,128)(2,1)} %sens_in.1, s32[1]{0:T(128)S(6)} %copy.14.count_in, s32[1,32]{1,0:T(1,128)} %spoke_index_in.1, s32[1,32]{1,0:T(1,128)} %offset_in.1, ...), custom_call_target="tpu_custom_call" | custom-call | tf_op jit(solution)/shard_map/pallas_call | solution.py:510
  29.6 1.6 %shard_map.131 = (f32[1,2048]{1,0:T(1,128)}, f32[1,2048]{1,0:T(1,128)}, bf16[1,2,128,256]{3,2,1,0:T(8,128)(2,1)}) custom-call(f32[1,2048]{1,0:T(1,128)} %get-tuple-element.6.refs_0_, f32[1,2048]{1,0:T(1,128)} %get-tuple-element.7.refs_1_, bf16[1,2,128,256]{3,2,1,0:T(8,128)(2,1)} %get-tuple-element.8.refs_2_), custom_call_target="tpu_custom_call" | custom-call | tf_op jit(solution)/shard_map/pallas_call | solution.py:556

commit v5 on v4

--- a/solution.py
+++ b/solution.py
@@ -88,10 +88,7 @@
     step_recv,
     res_send,
     res_recv,
-    steps,
-    pick_rows,
-    pick_send,
-    pick_recv,
+    own_hi,
     full,
     part_sems,
     raw_sems,
@@ -99,7 +96,6 @@
     img_sems,
     step_sems,
     res_sems,
-    pick_sems,
 ):
     _, coils, _, spokes, width = kspace.shape
     rows = owner_in.shape[1] // width
@@ -206,8 +202,7 @@
     par_start, par_wait, par_drain = exchange(par_send, par_recv, par_sems, *plane, True)
     img_start, img_wait, img_drain = exchange(img_send, img_recv, img_sems, *everyone, True)
     res_start, res_wait, res_drain = exchange(res_send, res_recv, res_sems, *everyone, True)
-    step_start, step_wait, step_drain = exchange(step_send, step_recv, step_sems, *plane, False)
-    pick_start, pick_wait, pick_drain = exchange(pick_send, pick_recv, pick_sems, *line, True)
+    step_start, step_wait, step_drain = exchange(step_send, step_recv, step_sems, *everyone, False)
 
     loaded("ktrans", "kep", "baseline")
     folds, fold = raw_rows.shape[0] // 4, raw_rows.shape[1]
@@ -301,7 +296,11 @@
     for c in range(1, n_coils):
         place = jnp.where(j == c, owner[c : c + 1, :], place)
     lo = place & (width - 1)
-    hi = lax.shift_right_logical(place, int(math.log2(width))) - z * plane_rows
+    hi = lax.shift_right_logical(place, int(math.log2(width)))
+    own_hi[...] = hi[:, :voxels]
+    for b in range(1, n_lines):
+        own_hi[...] = jnp.where(z == b, hi[:, b * voxels : (b + 1) * voxels], own_hi[...])
+    hi = hi - z * plane_rows
     for b in range(n_lines):
         cut = slice(b * voxels, (b + 1) * voxels)
         one_lo[:, cut] = jnp.where(
@@ -391,51 +390,32 @@
         ).astype(BF16)
     res_start()
 
-    def unpack(block, target, stride, number, planes):
+    def unpack(block, target, number):
         at = 0
-        for p in range(planes):
+        for p in range(2):
             for row, lanes in chunks.pieces(number):
-                top = p * stride + row
+                top = p * rows + row
                 target[top : top + chunks.rows, lanes] = block[at : at + chunks.rows]
                 at += chunks.rows
 
     step_wait()
-    for e in range(n_plane):
-        unpack(step_recv[e].astype(F32), steps, plane_rows, e, 2)
-    pick_folds, pick_fold = pick_rows.shape[0] // 2, pick_rows.shape[1]
-    for b in range(n_lines):
-        cut = slice(b * voxels, (b + 1) * voxels)
-        picked = jnp.dot(
-            steps[...].astype(BF16), one_lo[:, cut], preferred_element_type=F32
+    for e in range(n_frames):
+        unpack(step_recv[e].astype(F32), full, e)
+    own_cut = pl.ds(pl.multiple_of(z * voxels, LANES), voxels)
+    picked = jnp.dot(
+        full[...].astype(BF16), one_lo[:, own_cut], preferred_element_type=F32
+    )
+    in_row = lax.broadcasted_iota(jnp.int32, (rows, voxels), 0) == own_hi[...]
+    for p, (old, new) in enumerate(((ktrans, kt_out), (kep, kp_out))):
+        new[...] = old[...] + jnp.sum(
+            jnp.where(in_row, picked[p * rows : (p + 1) * rows], 0.0), 0, keepdims=True
         )
-        in_row = lax.broadcasted_iota(jnp.int32, (plane_rows, voxels), 0) == hi[:, cut]
-        for p in range(2):
-            chosen = jnp.sum(
-                jnp.where(in_row, picked[p * plane_rows : (p + 1) * plane_rows], 0.0),
-                0,
-                keepdims=True,
-            )
-            for i in range(pick_folds):
-                pick_rows[p * pick_folds + i : p * pick_folds + i + 1, :] = chosen[
-                    :, i * pick_fold : (i + 1) * pick_fold
-                ]
-        pick_send[b] = pick_rows[...].astype(BF16)
-    pick_start()
 
     res_wait()
     for e in range(n_frames):
-        unpack(res_recv[e].astype(F32), full, rows, e, 2)
+        unpack(res_recv[e].astype(F32), full, e)
     for p in range(2):
         res_out[0, p] = full[p * rows : (p + 1) * rows, :].astype(BF16)
-    pick_wait()
-    total = pick_recv[0].astype(F32)
-    for b in range(1, n_lines):
-        total = total + pick_recv[b].astype(F32)
-    for p, (old, new) in enumerate(((ktrans, kt_out), (kep, kp_out))):
-        for i in range(pick_folds):
-            cut = slice(i * pick_fold, (i + 1) * pick_fold)
-            row = p * pick_folds + i
-            new[:, cut] = old[:, cut] + total[row : row + 1]
     for k in range(1, n_coils):
         part_copy(k).wait_send()
     raw_drain()
@@ -443,7 +423,6 @@
     img_drain()
     step_drain()
     res_drain()
-    pick_drain()
 
 
 def hand_over(*refs):
@@ -487,7 +466,6 @@
     n_lines = n_frames // n_plane
     plane_rows = rows // n_lines
     folds = 4 if voxels % (4 * LANES) == 0 else 1
-    pick_folds = 8 if voxels % (8 * LANES) == 0 else 1
     vmem = pl.BlockSpec(memory_space=pltpu.VMEM)
     hbm = pl.BlockSpec(memory_space=pltpu.HBM)
     operands = (
@@ -533,21 +511,17 @@
             pltpu.VMEM((n_frames, 2 * height, LANES), BF16),
             pltpu.VMEM((n_frames, 2 * height, LANES), BF16),
             pltpu.VMEM((2 * height, LANES), BF16),
-            pltpu.VMEM((n_plane, 2 * height, LANES), BF16),
             pltpu.VMEM((n_frames, 2 * height, LANES), BF16),
             pltpu.VMEM((n_frames, 2 * height, LANES), BF16),
-            pltpu.VMEM((2 * plane_rows, width), F32),
-            pltpu.VMEM((2 * pick_folds, voxels // pick_folds), F32),
-            pltpu.VMEM((n_lines, 2 * pick_folds, voxels // pick_folds), BF16),
-            pltpu.VMEM((n_lines, 2 * pick_folds, voxels // pick_folds), BF16),
+            pltpu.VMEM((n_frames, 2 * height, LANES), BF16),
+            pltpu.VMEM((1, voxels), jnp.int32),
             pltpu.VMEM((2 * rows, width), F32),
             pltpu.SemaphoreType.DMA((2, n_coils)),
             pltpu.SemaphoreType.DMA((2, n_lines)),
             pltpu.SemaphoreType.DMA((2, n_plane)),
             pltpu.SemaphoreType.DMA((2, n_frames)),
-            pltpu.SemaphoreType.DMA((2, n_plane)),
             pltpu.SemaphoreType.DMA((2, n_frames)),
-            pltpu.SemaphoreType.DMA((2, n_lines)),
+            pltpu.SemaphoreType.DMA((2, n_frames)),
         ],
         compiler_params=pltpu.CompilerParams(
             collective_id=0, has_side_effects=True, vmem_limit_bytes=56 * 1024 * 1024

time: 31.5 us -> 29.6 us (0.940)
  Pallas kernels: 30 us -> 28.1 us
    pallas_call x1, Pallas kernels: 28.3 us -> 26.4 us  [shards(): pl.pallas_call(functools.partial(kernel, n_frames, n_coils), out_shape=[j...]
where the time goes in v5:
time: 29.6 us; the launch traced here: 29.3 us
  Pallas kernels  28.1 us (95%)
  between operations  1.29 us (4%)
    pallas_call x1, Pallas kernels, shards(): pl.pallas_call(functools.partial(kernel, n_frames, n_coils), out_shape=[j...  26.4 us
    pallas_call x1, Pallas kernels, shards(): pl.pallas_call(hand_over, out_shape=[jax.ShapeDtypeStruct(x.shape, x.dtyp...  1.65 us

profile of v5, /device:TPU:0, one launch (start us, length us, event | category | flops | bytes accessed | tf_op | source)
XLA Modules:
  0.0 29.3 jit_solution(17168347098707672872)
XLA Ops:
  1.3 26.4 %shard_map.130 = (f32[1,2048]{1,0:T(1,128)}, f32[1,2048]{1,0:T(1,128)}, bf16[1,2,128,256]{3,2,1,0:T(8,128)(2,1)}) custom-call(bf16[1,4,2,32,256]{4,3,2,1,0:T(8,128)(2,1)} %kspace_in.1, bf16[4,2,256,256]{3,2,1,0:T(8,128)(2,1)} %sens_in.1, s32[1]{0:T(128)S(6)} %copy.14.count_in, s32[1,32]{1,0:T(1,128)} %spoke_index_in.1, s32[1,32]{1,0:T(1,128)} %offset_in.1, ...), custom_call_target="tpu_custom_call" | custom-call | tf_op jit(solution)/shard_map/pallas_call | solution.py:488
  27.7 1.6 %shard_map.131 = (f32[1,2048]{1,0:T(1,128)}, f32[1,2048]{1,0:T(1,128)}, bf16[1,2,128,256]{3,2,1,0:T(8,128)(2,1)}) custom-call(f32[1,2048]{1,0:T(1,128)} %get-tuple-element.6.refs_0_, f32[1,2048]{1,0:T(1,128)} %get-tuple-element.7.refs_1_, bf16[1,2,128,256]{3,2,1,0:T(8,128)(2,1)} %get-tuple-element.8.refs_2_), custom_call_target="tpu_custom_call" | custom-call | tf_op jit(solution)/shard_map/pallas_call | solution.py:530

commit v6 on v5

--- a/solution.py
+++ b/solution.py
@@ -210,8 +210,6 @@
         for i in range(folds):
             raw_rows[p * folds + i : p * folds + i + 1, :] = value[:, i * fold : (i + 1) * fold]
     raw_send[...] = raw_rows[...].astype(BF16)
-    pl.semaphore_wait(barrier, n_frames + n_coils - 2)
-    raw_start()
 
     loaded("index", "offset", "count", "table")
     number = spoke_index[...]
@@ -289,7 +287,12 @@
         image_r, image_i = partial(coil_peer(k))
         part_send[k - 1, 0] = image_r
         part_send[k - 1, 1] = image_i
+    pl.semaphore_wait(barrier, n_frames + n_coils - 2)
+    for k in range(1, n_coils):
         part_copy(k).start()
+    raw_start()
+
+    image_r, image_i = partial(j)
 
     loaded(*range(n_lines))
     place = owner[0:1, :]
@@ -306,6 +309,16 @@
         one_lo[:, cut] = jnp.where(
             lax.broadcasted_iota(jnp.int32, (width, voxels), 0) == lo[:, cut], 1.0, 0.0
         ).astype(BF16)
+
+    for k in range(1, n_coils):
+        part_copy(k).wait_recv()
+        image_r = image_r + part_recv[k - 1, 0]
+        image_i = image_i + part_recv[k - 1, 1]
+    for e in range(n_frames):
+        pieces = chunks.take(image_r, e) + chunks.take(image_i, e)
+        img_send[e] = jnp.concatenate(pieces, 0).astype(BF16)
+    img_start()
+
     raw_wait()
     for b in range(n_lines):
         block = raw_recv[b].astype(F32)
@@ -327,15 +340,6 @@
         par_send[e] = jnp.concatenate(pieces, 0).astype(BF16)
     par_start()
 
-    image_r, image_i = partial(j)
-    for k in range(1, n_coils):
-        part_copy(k).wait_recv()
-        image_r = image_r + part_recv[k - 1, 0]
-        image_i = image_i + part_recv[k - 1, 1]
-    for e in range(n_frames):
-        pieces = chunks.take(image_r, e) + chunks.take(image_i, e)
-        img_send[e] = jnp.concatenate(pieces, 0).astype(BF16)
-    img_start()
 
     par_wait()
     params = par_recv[0].astype(F32)

time: 29.6 us -> 27.3 us (0.922)
  Pallas kernels: 28.1 us -> 25.8 us
    pallas_call x1, Pallas kernels: 26.4 us -> 24.1 us  [shards(): pl.pallas_call(functools.partial(kernel, n_frames, n_coils), out_shape=[j...]
where the time goes in v6:
time: 27.3 us; the launch traced here: 27.1 us
  Pallas kernels  25.8 us (95%)
  between operations  1.29 us (5%)
    pallas_call x1, Pallas kernels, shards(): pl.pallas_call(functools.partial(kernel, n_frames, n_coils), out_shape=[j...  24.1 us
    pallas_call x1, Pallas kernels, shards(): pl.pallas_call(hand_over, out_shape=[jax.ShapeDtypeStruct(x.shape, x.dtyp...  1.65 us

profile of v6, /device:TPU:0, one launch (start us, length us, event | category | flops | bytes accessed | tf_op | source)
XLA Modules:
  0.0 27.1 jit_solution(15103179105523468011)
XLA Ops:
  1.3 24.1 %shard_map.130 = (f32[1,2048]{1,0:T(1,128)}, f32[1,2048]{1,0:T(1,128)}, bf16[1,2,128,256]{3,2,1,0:T(8,128)(2,1)}) custom-call(bf16[1,4,2,32,256]{4,3,2,1,0:T(8,128)(2,1)} %kspace_in.1, bf16[4,2,256,256]{3,2,1,0:T(8,128)(2,1)} %sens_in.1, s32[1]{0:T(128)S(6)} %copy.14.count_in, s32[1,32]{1,0:T(1,128)} %spoke_index_in.1, s32[1,32]{1,0:T(1,128)} %offset_in.1, ...), custom_call_target="tpu_custom_call" | custom-call | tf_op jit(solution)/shard_map/pallas_call | solution.py:492
  25.4 1.6 %shard_map.131 = (f32[1,2048]{1,0:T(1,128)}, f32[1,2048]{1,0:T(1,128)}, bf16[1,2,128,256]{3,2,1,0:T(8,128)(2,1)}) custom-call(f32[1,2048]{1,0:T(1,128)} %get-tuple-element.6.refs_0_, f32[1,2048]{1,0:T(1,128)} %get-tuple-element.7.refs_1_, bf16[1,2,128,256]{3,2,1,0:T(8,128)(2,1)} %get-tuple-element.8.refs_2_), custom_call_target="tpu_custom_call" | custom-call | tf_op jit(solution)/shard_map/pallas_call | solution.py:534

commit v7 on v6

--- a/solution.py
+++ b/solution.py
@@ -211,7 +211,7 @@
             raw_rows[p * folds + i : p * folds + i + 1, :] = value[:, i * fold : (i + 1) * fold]
     raw_send[...] = raw_rows[...].astype(BF16)
 
-    loaded("index", "offset", "count", "table")
+    loaded("index", "offset", "count", "table", "kspace")
     number = spoke_index[...]
     turn = ((number * 40503) & 65535).astype(F32) * (2.0 * math.pi / 65536.0)
     live = jnp.where(
@@ -240,7 +240,6 @@
         + lax.dot_general(table[:, width:], m_b, NT, preferred_element_type=F32)
     ).astype(BF16)
 
-    loaded("kspace")
     lines = jnp.dot(
         kspace[0].reshape(coils * 2 * spokes, width), table[...], preferred_element_type=F32
     )
@@ -332,7 +331,7 @@
                 ],
                 0,
             ).astype(BF16)
-    placed = lax.dot_general(spread[...], one_lo[...], NT, preferred_element_type=F32)
+    placed = lax.dot_general(one_lo[...], spread[...], NT, preferred_element_type=F32).T
     for e in range(n_plane):
         pieces = []
         for p in range(4):

time: 27.3 us -> 27.4 us (level)
  no operation moved by 1% of the time
where the time goes in v7:
time: 27.4 us; the launch traced here: 27.1 us
  Pallas kernels  25.9 us (95%)
  between operations  1.29 us (5%)
    pallas_call x1, Pallas kernels, shards(): pl.pallas_call(functools.partial(kernel, n_frames, n_coils), out_shape=[j...  24.2 us
    pallas_call x1, Pallas kernels, shards(): pl.pallas_call(hand_over, out_shape=[jax.ShapeDtypeStruct(x.shape, x.dtyp...  1.65 us

profile of v7, /device:TPU:0, one launch (start us, length us, event | category | flops | bytes accessed | tf_op | source)
XLA Modules:
  0.0 27.1 jit_solution(6085803332016896257)
XLA Ops:
  1.3 24.2 %shard_map.130 = (f32[1,2048]{1,0:T(1,128)}, f32[1,2048]{1,0:T(1,128)}, bf16[1,2,128,256]{3,2,1,0:T(8,128)(2,1)}) custom-call(bf16[1,4,2,32,256]{4,3,2,1,0:T(8,128)(2,1)} %kspace_in.1, bf16[4,2,256,256]{3,2,1,0:T(8,128)(2,1)} %sens_in.1, s32[1]{0:T(128)S(6)} %copy.14.count_in, s32[1,32]{1,0:T(1,128)} %spoke_index_in.1, s32[1,32]{1,0:T(1,128)} %offset_in.1, ...), custom_call_target="tpu_custom_call" | custom-call | tf_op jit(solution)/shard_map/pallas_call | solution.py:491
  25.5 1.6 %shard_map.131 = (f32[1,2048]{1,0:T(1,128)}, f32[1,2048]{1,0:T(1,128)}, bf16[1,2,128,256]{3,2,1,0:T(8,128)(2,1)}) custom-call(f32[1,2048]{1,0:T(1,128)} %get-tuple-element.6.refs_0_, f32[1,2048]{1,0:T(1,128)} %get-tuple-element.7.refs_1_, bf16[1,2,128,256]{3,2,1,0:T(8,128)(2,1)} %get-tuple-element.8.refs_2_), custom_call_target="tpu_custom_call" | custom-call | tf_op jit(solution)/shard_map/pallas_call | solution.py:533

commit v8 on v5

--- a/solution.py
+++ b/solution.py
@@ -210,8 +210,6 @@
         for i in range(folds):
             raw_rows[p * folds + i : p * folds + i + 1, :] = value[:, i * fold : (i + 1) * fold]
     raw_send[...] = raw_rows[...].astype(BF16)
-    pl.semaphore_wait(barrier, n_frames + n_coils - 2)
-    raw_start()
 
     loaded("index", "offset", "count", "table")
     number = spoke_index[...]
@@ -289,7 +287,12 @@
         image_r, image_i = partial(coil_peer(k))
         part_send[k - 1, 0] = image_r
         part_send[k - 1, 1] = image_i
+    pl.semaphore_wait(barrier, n_frames + n_coils - 2)
+    for k in range(1, n_coils):
         part_copy(k).start()
+    raw_start()
+
+    image_r, image_i = partial(j)
 
     loaded(*range(n_lines))
     place = owner[0:1, :]
@@ -306,6 +309,7 @@
         one_lo[:, cut] = jnp.where(
             lax.broadcasted_iota(jnp.int32, (width, voxels), 0) == lo[:, cut], 1.0, 0.0
         ).astype(BF16)
+
     raw_wait()
     for b in range(n_lines):
         block = raw_recv[b].astype(F32)
@@ -327,7 +331,6 @@
         par_send[e] = jnp.concatenate(pieces, 0).astype(BF16)
     par_start()
 
-    image_r, image_i = partial(j)
     for k in range(1, n_coils):
         part_copy(k).wait_recv()
         image_r = image_r + part_recv[k - 1, 0]

time: 29.6 us -> 29.1 us (0.983)
  Pallas kernels: 28.1 us -> 27.5 us
    pallas_call x1, Pallas kernels: 26.4 us -> 25.9 us  [shards(): pl.pallas_call(functools.partial(kernel, n_frames, n_coils), out_shape=[j...]
where the time goes in v8:
time: 29.1 us; the launch traced here: 28.8 us
  Pallas kernels  27.5 us (95%)
  between operations  1.29 us (4%)
    pallas_call x1, Pallas kernels, shards(): pl.pallas_call(functools.partial(kernel, n_frames, n_coils), out_shape=[j...  25.9 us
    pallas_call x1, Pallas kernels, shards(): pl.pallas_call(hand_over, out_shape=[jax.ShapeDtypeStruct(x.shape, x.dtyp...  1.65 us

profile of v8, /device:TPU:0, one launch (start us, length us, event | category | flops | bytes accessed | tf_op | source)
XLA Modules:
  0.0 28.8 jit_solution(8809784625014391284)
XLA Ops:
  1.3 25.9 %shard_map.130 = (f32[1,2048]{1,0:T(1,128)}, f32[1,2048]{1,0:T(1,128)}, bf16[1,2,128,256]{3,2,1,0:T(8,128)(2,1)}) custom-call(bf16[1,4,2,32,256]{4,3,2,1,0:T(8,128)(2,1)} %kspace_in.1, bf16[4,2,256,256]{3,2,1,0:T(8,128)(2,1)} %sens_in.1, s32[1]{0:T(128)S(6)} %copy.14.count_in, s32[1,32]{1,0:T(1,128)} %spoke_index_in.1, s32[1,32]{1,0:T(1,128)} %offset_in.1, ...), custom_call_target="tpu_custom_call" | custom-call | tf_op jit(solution)/shard_map/pallas_call | solution.py:491
  27.2 1.6 %shard_map.131 = (f32[1,2048]{1,0:T(1,128)}, f32[1,2048]{1,0:T(1,128)}, bf16[1,2,128,256]{3,2,1,0:T(8,128)(2,1)}) custom-call(f32[1,2048]{1,0:T(1,128)} %get-tuple-element.6.refs_0_, f32[1,2048]{1,0:T(1,128)} %get-tuple-element.7.refs_1_, bf16[1,2,128,256]{3,2,1,0:T(8,128)(2,1)} %get-tuple-element.8.refs_2_), custom_call_target="tpu_custom_call" | custom-call | tf_op jit(solution)/shard_map/pallas_call | solution.py:533
